TPU v7x, 512 devices: a whole 4x4x16 slice. The times are simulated.
512 devices in a mesh: row: 128 (over z, y, core), head: 4 (over x).
Axes of the slice: x: 4, y: 4, z: 16, core: 2. Of those that a mesh axis runs over, the one named last changes fastest.
Arguments:
- residual: bfloat16 [3072, 2048], P('row'), may hold values from -3 to 3
- queries: bfloat16 [3072, 1024], P('row', 'head'), may hold values from -6 to 6
- keys: bfloat16 [3072, 1024], P('row', 'head'), may hold values from -6 to 6
- values: bfloat16 [3072, 2048], P('row', 'head'), may hold values from -6 to 6
- out_gate: bfloat16 [3072, 2048], P('row', 'head'), may hold values from -6 to 6
- decay_input: float32 [3072, 16], P('row', 'head'), may hold values from -4 to 4
- beta_input: float32 [3072, 16], P('row', 'head'), may hold values from -6 to 6
- decay_log: float32 [16], P('head'), may hold values from -1.5 to 1.5
- decay_bias: float32 [16], P('head'), may hold values from -1 to 1
- past_state: bfloat16 [3072, 16, 128, 128], P('row', 'head'), may hold values from -2 to 2
- head_norm: float32 [128], replicated, may hold values from 0.1 to 1.9
- out_proj: bfloat16 [2048, 2048], P('head'), may hold values from -0.125 to 0.125
- post_norm: float32 [2048], replicated, may hold values from 0.1 to 1.9
- expert_ids: int32 [3072, 10], P('row'), may hold values from 0 to 255, as said below
- expert_gates: float32 [3072, 10], P('row'), may hold values from 0.1 to 1
- capacity: int32 [256], replicated, may hold values from 60 to 239
- gate_proj: bfloat16 [128, 2048, 512], P('row', None, 'head'), may hold values from -0.125 to 0.125
- up_proj: bfloat16 [128, 2048, 512], P('row', None, 'head'), may hold values from -0.125 to 0.125
- down_proj: bfloat16 [128, 512, 2048], P('row', 'head'), may hold values from -0.375 to 0.375
Outputs:
- mixed: bfloat16 [3072, 2048], P(('row', 'head'))
Inputs may be any that keep to these rules, and one draw needn't show every extreme that they name: `expert_ids`: each row names 10 different experts. Among the rows of one index of row no expert is named by more than 2 rows, and some expert by exactly 2. Counts of choices may travel packed several to a 32-bit word.
All inputs are finite; a program needn't handle non-finite values.
Results may differ from a plain program's by a relative error of at most 0.0085.
Values may be sent and summed in bfloat16 or wider, within the bound.
A program may use at most 64 MiB of HBM per device.

v0:
```python
import jax
import jax.numpy as jnp
from jax import lax
from jax.sharding import PartitionSpec as P

DK = 128
DV = 128
TOPK = 10


def prefix(part, axis, combine, identity):
    place = lax.axis_index(axis)
    gathered = lax.all_gather(part, axis)
    state = jnp.zeros_like(part) + jnp.asarray(identity, part.dtype)

    def one(step, state):
        return combine(state, lax.dynamic_index_in_dim(gathered, step, 0, False))

    return lax.fori_loop(0, place, one, state)


def unit_rows(block):
    return block * lax.rsqrt(jnp.sum(block * block, axis=-1, keepdims=True) + 1e-06)


def scaled_rms(block, weight):
    return block * lax.rsqrt(jnp.mean(block * block, axis=-1, keepdims=True) + 1e-06) * weight


def add_counts(earlier, later):
    return earlier + later


def expert_rows(received, gate_proj, up_proj, down_proj):
    layout = received.shape
    flat = received.reshape(-1, layout[-1])
    gate_val = jnp.dot(flat, gate_proj[0], preferred_element_type=jnp.float32)
    up_val = jnp.dot(flat, up_proj[0], preferred_element_type=jnp.float32)
    inner = (jax.nn.silu(gate_val) * up_val).astype(jnp.bfloat16)
    part_out = jnp.dot(inner, down_proj[0], preferred_element_type=jnp.float32).astype(jnp.bfloat16)
    return lax.all_to_all(part_out.reshape(layout), "row", split_axis=0, concat_axis=0, tiled=True)


def on_device(
    residual,
    queries,
    keys,
    values,
    out_gate,
    decay_input,
    beta_input,
    decay_log,
    decay_bias,
    past_state,
    head_norm,
    out_proj,
    post_norm,
    expert_ids,
    expert_gates,
    capacity,
    gate_proj,
    up_proj,
    down_proj,
):
    rows = residual.shape[0]
    width = residual.shape[1]
    heads = values.shape[1] // DV
    groups = queries.shape[1] // DK
    ratio = heads // groups
    quarter = rows // lax.axis_size("head")
    head_pos = lax.axis_index("head")
    row_devices = lax.axis_size("row")
    experts = 2 * row_devices
    most = max(2, min(rows, 2 * ((rows * TOPK + 2 * experts - 1) // (2 * experts))))
    q_unit = unit_rows(queries.astype(jnp.float32).reshape(rows, groups, DK)) * DK ** (-0.5)
    k_unit = unit_rows(keys.astype(jnp.float32).reshape(rows, groups, DK))
    paired_qk = jnp.repeat(jnp.stack([q_unit, k_unit], axis=2), ratio, axis=1)
    reads = jnp.einsum(
        "rhij,rhci->rhcj",
        past_state.astype(jnp.float32),
        paired_qk,
        precision=lax.Precision.HIGHEST,
    )
    decay = jnp.exp(
        -jnp.exp(decay_log)[None, :] * jax.nn.softplus(decay_input + decay_bias[None, :])
    )[:, :, None]
    beta = jax.nn.sigmoid(beta_input)[:, :, None]
    value_all = values.astype(jnp.float32).reshape(rows, heads, DV)
    update = beta * (value_all - decay * reads[:, :, 1])
    intersection_qk = jnp.sum(paired_qk[:, :, 0] * paired_qk[:, :, 1], axis=-1, keepdims=True)
    head_out = decay * reads[:, :, 0] + intersection_qk * update
    gate_all = out_gate.astype(jnp.float32).reshape(rows, heads, DV)
    gated = (
        (scaled_rms(head_out, head_norm) * jax.nn.silu(gate_all))
        .astype(jnp.bfloat16)
        .reshape(rows, heads * DV)
    )
    attn = lax.psum(jnp.dot(gated, out_proj, preferred_element_type=jnp.float32), "head")
    stream = residual.astype(jnp.float32) + attn
    normed = scaled_rms(stream, post_norm).astype(jnp.bfloat16)
    kept_stream = lax.dynamic_slice_in_dim(stream, head_pos * quarter, quarter, 0)
    flat_ids = expert_ids.reshape(-1)
    picks = (flat_ids[:, None] == jnp.arange(experts, dtype=jnp.int32)[None, :]).astype(jnp.int32)
    counts = jnp.sum(picks, axis=0)
    before = prefix(counts, "row", add_counts, jnp.zeros_like(counts))
    local_rank = jnp.sum((jnp.cumsum(picks, axis=0) - picks) * picks, axis=1)
    global_rank = local_rank + jnp.sum(picks * before[None, :], axis=1)
    limit = jnp.sum(picks * capacity[None, :], axis=1)
    kept_gate = jnp.where(global_rank < limit, expert_gates.reshape(-1), 0.0)
    parity = head_pos // 2
    slots = row_devices * most
    slot_id = jnp.where(flat_ids % 2 == parity, flat_ids // 2 * most + local_rank, -1)
    hits = (slot_id[:, None] == jnp.arange(slots, dtype=jnp.int32)[None, :]).astype(jnp.float32)
    row_hits = jnp.sum(hits.reshape(rows, TOPK, slots), axis=1).astype(jnp.bfloat16)
    combine_table = jnp.sum((hits * kept_gate[:, None]).reshape(rows, TOPK, slots), axis=1)
    outgoing = lax.dot_general(
        row_hits, normed, (((0,), (0,)), ((), ())), preferred_element_type=jnp.float32
    )
    outgoing = outgoing.astype(jnp.bfloat16).reshape(row_devices, most, width)
    returned = expert_rows(
        lax.all_to_all(outgoing, "row", split_axis=0, concat_axis=0, tiled=True),
        gate_proj,
        up_proj,
        down_proj,
    )
    returned_flat = returned.reshape(slots, width).astype(jnp.float32)
    moe_rows = lax.psum_scatter(
        jnp.dot(combine_table, returned_flat, precision=lax.Precision.HIGHEST),
        "head",
        scatter_dimension=0,
        tiled=True,
    )
    return (kept_stream + moe_rows).astype(jnp.bfloat16)


def solution(mesh):
    placed = (
        P("row", None),
        P("row", "head"),
        P("row", "head"),
        P("row", "head"),
        P("row", "head"),
        P("row", "head"),
        P("row", "head"),
        P("head"),
        P("head"),
        P("row", "head", None, None),
        P(),
        P("head", None),
        P(),
        P("row", None),
        P("row", None),
        P(),
        P("row", None, "head"),
        P("row", None, "head"),
        P("row", "head", None),
    )
    return jax.shard_map(
        on_device, mesh=mesh, in_specs=placed, out_specs=P(("row", "head"), None), check_vma=False
    )
```

profile of v0, /device:TPU:6, one launch (start us, length us, event | category | flops | bytes accessed | tf_op | source)
XLA Modules:
  0.0 286.2 jit_solution(7123530486795170455)
XLA Ops:
  6.5 0.9 reshape.198
  7.4 0.8 convert_multiply_fusion.2
  8.2 0.7 reshape.199
  8.9 0.7 convert_multiply_fusion.1
  9.6 0.8 reshape.201
  10.4 0.1 reduce_sum.105
  10.6 0.1 reduce_sum.106
  10.7 0.1 multiply_multiply_fusion
  11.0 0.2 fusion.29
  11.3 2.5 fusion.48
  13.8 0.2 slice_reduce_fusion
  14.0 0.1 copy.53
  14.2 0.1 copy.50
  14.3 0.2 multiply_reduce_fusion.1
  14.7 0.1 mul.233
  14.8 0.1 mul.231
  14.9 0.1 mul.217
  15.0 2.7 fusion.31
  17.7 0.1 copy.54
  17.8 0.1 eq.51
  17.9 0.1 convert_reduce_fusion
  18.0 0.1 iota_compare_fusion.1
  18.1 89.5 %all-gather.1 = s32[128,1,256]{2,1,0:T(1,128)S(1)} all-gather(s32[1,1,256]{2,1,0:T(1,128)S(1)} %bitcast.115), channel_id=2, replica_groups=mesh['row'=128,'head'=4] {'row'}, dimensions={0}, use_global_device_ids=true | all-gather | bytes 132096 | tf_op jit(solution)/shard_map/all_gather | solution.py:13
  107.7 0.2 fusion.8
  108.1 0.3 select_reduce_fusion.2
  108.3 0.1 reduce_sum.110
  108.5 0.1 copy.62
  108.5 0.1 reduce_sum.115
  108.6 0.1 reduce_sum.113
  108.9 0.7 convert_reduce_fusion.1
  109.7 1.1 multiply_reduce_fusion
  110.8 1.5 convolution_convert_fusion.1
  112.3 2.5 reshape.204
  114.8 67.9 %all_to_all.10 = bf16[128,2,2048]{2,1,0:T(2,128)(2,1)} all-to-all(bf16[128,2,2048]{2,1,0:T(2,128)(2,1)} %reshape.204), channel_id=1, replica_groups=mesh['row'=128,'head'=4] {'row'}, dimensions={0} | all-to-all | bytes 2097152 | tf_op jit(solution)/shard_map/all_to_all | solution.py:121
  182.7 2.3 reshape.205
  185.0 1.8 fusion.5
  186.7 3.3 %convolution_convert_fusion = bf16[256,2048]{1,0:T(8,128)(2,1)} fusion(bf16[256,2048]{1,0:T(8,128)(2,1)} %reshape.205, bf16[1,128,2048]{2,1,0:T(8,128)(2,1)} %param.39, bf16[1,2048,128]{2,1,0:T(8,128)(2,1)} %param.38, f32[256,128]{1,0:T(8,128)S(1)} %fusion.5), kind=kOutput, calls=%fused_computation.1 | convolution fusion | flops 269156352 | bytes 3276800 | tf_op jit(solution)/shard_map/dot_general | solution.py:40
  190.1 2.5 reshape.206
  192.6 62.2 %all_to_all.11 = bf16[128,2,2048]{2,1,0:T(2,128)(2,1)} all-to-all(bf16[128,2,2048]{2,1,0:T(2,128)(2,1)} %reshape.206), channel_id=1, replica_groups=mesh['row'=128,'head'=4] {'row'}, dimensions={0} | all-to-all | bytes 2097152 | tf_op jit(solution)/shard_map/all_to_all | solution.py:41
  254.8 2.3 reshape.207
  257.0 1.8 fusion.49
  258.8 12.0 %fusion = f32[8,2048]{1,0:T(8,128)} fusion(f32[24,2048]{1,0:T(8,128)S(1)} %fusion.49), kind=kCustom, calls=%all-reduce-scatter | all-reduce-scatter fusion | flops 65537 | bytes 264192
  270.8 0.8 slice.35
  271.6 1.3 collective-permute-start
  272.9 1.3 dynamic-slice.4
  274.8 2.9 %collective-permute-done = f32[6,2048]{1,0:T(8,128)S(1)} collective-permute-done((f32[6,2048]{1,0:T(8,128)S(1)}, f32[6,2048]{1,0:T(8,128)S(1)}, u32[]{:S(2)}, u32[]{:S(2)}) %collective-permute-start) | collective-permute-done | bytes 49184
  277.8 1.0 concatenate
  278.8 0.6 fusion.18
  (57 shorter events, 0.7 us)
Async XLA Ops:
  6.5 4.7 %copy-start = (bf16[24,4,128,128]{3,2,1,0:T(8,128)(2,1)S(1)}, bf16[24,4,128,128]{3,2,1,0:T(8,128)(2,1)}, u32[]{:S(2)}) copy-start(bf16[24,4,128,128]{3,2,1,0:T(8,128)(2,1)} %param.30) | copy-start | bytes 9437188
  6.5 103.2 %all-reduce.5.cloned.1.call-start = ((), (), s32[]{:S(2)}) async-start(), calls=%async_computation.2 | async-start | bytes 393216 | tf_op jit(solution)/shard_map/psum | solution.py:98
  10.7 3.3 %copy-start.7 = (f32[24,4]{0,1:T(4,128)S(1)}, f32[24,4]{0,1:T(4,128)}, u32[]{:S(2)}) copy-start(f32[24,4]{0,1:T(4,128)} %param.27) | copy-start | bytes 1156
  10.7 3.4 %copy-start.12 = (f32[4]{0:T(128)S(1)}, f32[4]{0:T(128)}, u32[]{:S(2)}) copy-start(f32[4]{0:T(128)} %param.28) | copy-start | bytes 52
  10.7 3.4 %copy-start.8 = (f32[24,4]{0,1:T(4,128)S(1)}, f32[24,4]{0,1:T(4,128)}, u32[]{:S(2)}) copy-start(f32[24,4]{0,1:T(4,128)} %param.26) | copy-start | bytes 1156
  10.7 3.4 %copy-start.10 = (f32[4]{0:T(128)S(1)}, f32[4]{0:T(128)}, u32[]{:S(2)}) copy-start(f32[4]{0:T(128)} %param.29) | copy-start | bytes 52
  10.9 3.7 %copy-start.11 = (f32[128]{0:T(128)S(1)}, f32[128]{0:T(128)}, u32[]{:S(2)}) copy-start(f32[128]{0:T(128)} %param.31) | copy-start | bytes 1540
  11.0 4.0 %copy-start.1 = (bf16[24,512]{1,0:T(8,128)(2,1)S(1)}, bf16[24,512]{1,0:T(8,128)(2,1)}, u32[]{:S(2)}) copy-start(bf16[24,512]{1,0:T(8,128)(2,1)} %param.24) | copy-start | bytes 73732
  11.0 4.0 %copy-start.3 = (bf16[24,512]{1,0:T(8,128)(2,1)S(1)}, bf16[24,512]{1,0:T(8,128)(2,1)}, u32[]{:S(2)}) copy-start(bf16[24,512]{1,0:T(8,128)(2,1)} %param.25) | copy-start | bytes 73732
  13.8 3.9 %copy-start.5 = (s32[24,10]{0,1:T(8,128)S(1)}, s32[24,10]{0,1:T(8,128)}, u32[]{:S(2)}) copy-start(s32[24,10]{0,1:T(8,128)} %param.34) | copy-start | bytes 2884
  17.7 90.4 %copy-start.9 = (s32[256]{0:T(256)S(1)}, s32[256]{0:T(256)}, u32[]{:S(2)}) copy-start(s32[256]{0:T(256)} %param.36) | copy-start | bytes 3076
  17.7 90.8 %copy-start.6 = (f32[24,10]{0,1:T(8,128)S(1)}, f32[24,10]{0,1:T(8,128)}, u32[]{:S(2)}) copy-start(f32[24,10]{0,1:T(8,128)} %param.35) | copy-start | bytes 2884
  17.7 92.0 %copy-start.2 = (bf16[24,2048]{1,0:T(8,128)(2,1)S(1)}, bf16[24,2048]{1,0:T(8,128)(2,1)}, u32[]{:S(2)}) copy-start(bf16[24,2048]{1,0:T(8,128)(2,1)} %param.21) | copy-start | bytes 294916
  17.7 93.1 %copy-start.4 = (f32[2048]{0:T(1024)S(1)}, f32[2048]{0:T(1024)}, u32[]{:S(2)}) copy-start(f32[2048]{0:T(1024)} %param.33) | copy-start | bytes 24580
  271.6 6.1 %collective-permute-start = (f32[6,2048]{1,0:T(8,128)S(1)}, f32[6,2048]{1,0:T(8,128)S(1)}, u32[]{:S(2)}, u32[]{:S(2)}) collective-permute-start(f32[6,2048]{1,0:T(8,128)S(1)} %slice.35), channel_id=1, source_target_pairs={{0,1},{1,2},{2,3},{4,5},{5,6},{6,7},{8,9},{9,10},{10,11},{12,13},{... | collective-permute-start | bytes 147464
Sparse Core Ops, SparseCore 0:
  17.8 60.1 all-reduce.4
where the time goes:
time: 290 us; the launch traced here: 286 us
  blocking collectives  232 us (80%)
  local copies, waits for them, and re-layouts  16.6 us (6%)
  between operations  14.5 us (5%)
  matrix products  13.6 us (5%)
  other arithmetic  5.73 us (2%)
  waiting for transfers between devices  2.95 us (1%)
    all_gather x1, blocking collectives, prefix(): gathered = lax.all_gather(part, axis)  89.5 us
    all_to_all x1, blocking collectives, on_device(): lax.all_to_all(outgoing, 'row', split_axis=0, concat_axis=0, tiled=True)  67.9 us
    all_to_all x1, blocking collectives, expert_rows(): lax.all_to_all(part_out.reshape(layout), 'row', split_axis=0, concat_axis...  62.2 us
    unnamed x1, blocking collectives  12 us
  transfers between devices with their start and end apart: 2, of which 1 were waited for; matrix products, arithmetic and copies ran while one was open for 1% of the time, Pallas kernels for 0%

commit v1 on v0

v1 whole, which is shorter than its diff:
```python
import jax
import jax.numpy as jnp
from jax import lax
from jax.experimental import pallas as pl
from jax.experimental.pallas import tpu as pltpu
from jax.sharding import PartitionSpec as P

MESH = pl.DeviceIdType.MESH
BF = jnp.bfloat16
F32 = jnp.float32
HIGH = lax.Precision.HIGHEST

ROWS = 24
TOPK = 10
HEADS = 4
DX = 512
CH, CW = 48, 256
STEP = 4

ORDER = (0, -1, 1, -2, 2, -3, 3, -4, 4, -5, 5, -6, 6, -7, 7, -8)
PLACE = {delta: place for place, delta in enumerate(ORDER)}
DIRECT = (-6, 5, -3, 3, -1, 1)
RELAY = {-2: -1, 2: 1, -4: -3, -5: -3, 4: 3, 6: 5, 7: 5, -7: -6, -8: -6}
REACH = (-6, -5, -3, -2, -1, 1, 2, 3, 5, 6)
N_SEM = 128


def dot(a, b):
    return jnp.dot(a, b, preferred_element_type=F32)


def iota(shape, dim):
    return lax.broadcasted_iota(jnp.int32, shape, dim)


def sigmoid(v):
    return 1.0 / (1.0 + jnp.exp(-v))


def kernel(
    res_ref, q_ref, k_ref, v_ref, og_ref, di_ref, bi_ref, dl_ref, db_ref, hn_ref, pn_ref,
    ids_ref, eg_ref, cap_ref, state_hbm, op_hbm, gp_hbm, up_hbm, dp_hbm,
    out_ref,
    ST, OP, W, D, MG, AQ, RD, AP, AR, SM, G, PTL, PTR, PL, PR, S, R, GM, GS, KW,
    MS, MR, SSB, SSR, IN, Y, R2, C, CB, T, FX, FO,
    ss, rs, ls,
):
    row = lax.axis_index("row")
    x = lax.axis_index("head")
    z = row // 8
    me = row % 8
    xs = [x] + [(x + k) % 4 for k in range(1, 4)]
    ds = [me] + [(me + k) % 8 for k in range(1, 8)]

    def at_z(off):
        return (((z + 16 + off) % 16) * 8 + me, x)

    def at_y(k):
        return (z * 8 + ds[k], x)

    def at_x(k):
        return (row, xs[k])

    sent = []

    def remote(src, dst, device):
        n = len(sent)
        copy = pltpu.make_async_remote_copy(
            src_ref=src, dst_ref=dst, send_sem=ss.at[n], recv_sem=rs.at[n], device_id=device, device_id_type=MESH
        )
        copy.start()
        sent.append(copy)
        return copy

    n_local = [0]

    def local(src, dst):
        copy = pltpu.make_async_copy(src, dst, ls.at[n_local[0]])
        n_local[0] += 1
        copy.start()
        return copy

    def x_cols(k):
        return pl.ds(pl.multiple_of(xs[k] * DX, DX), DX)

    states = [local(state_hbm.at[pl.ds(STEP * i, STEP)], ST.at[pl.ds(STEP * i, STEP)]) for i in range(ROWS // STEP)]
    projs = [local(op_hbm.at[:, x_cols(k)], OP.at[k]) for k in (2, 1, 3, 0)]
    own_w = [
        local(gp_hbm.at[0, x_cols(0), :], W.at[x, :, pl.ds(0, 128)]),
        local(up_hbm.at[0, x_cols(0), :], W.at[x, :, pl.ds(128, 128)]),
        local(dp_hbm.at[0, :, x_cols(0)], D.at[x]),
    ]

    barrier = pltpu.get_barrier_semaphore()
    peers = [at_z(off) for off in REACH] + [at_y(k) for k in range(1, 8)] + [at_x(k) for k in range(1, 4)]
    for device in peers:
        pl.semaphore_signal(barrier, inc=1, device_id=device, device_id_type=MESH)
    pl.semaphore_wait(barrier, len(peers))

    def direct(buf):
        return {a: remote(buf.at[0], buf.at[PLACE[a]], at_z(-a)) for a in DIRECT}

    def relay(buf, copies, via):
        copies[via].wait_recv()
        for delta, v in RELAY.items():
            if v == via:
                copies[delta] = remote(buf.at[PLACE[v]], buf.at[PLACE[delta]], at_z(v - delta))

    MG[0] = jnp.concatenate([ids_ref[...].astype(F32), eg_ref[...], jnp.zeros((ROWS, 128 - 2 * TOPK), F32)], axis=1)
    meta = direct(MG)

    moved_w = []
    for k in (2, 1, 3):
        moved_w.append(remote(gp_hbm.at[0, x_cols(k), :], W.at[x, :, pl.ds(0, 128)], at_x(k)))
        moved_w.append(remote(up_hbm.at[0, x_cols(k), :], W.at[x, :, pl.ds(128, 128)], at_x(k)))

    q_unit, k_unit, cross = [], [], []
    for g in range(2):
        for ref, scale, units, base in ((q_ref, 128 ** (-0.5), q_unit, 0), (k_ref, 1.0, k_unit, 2)):
            block = ref[:, 128 * g : 128 * g + 128].astype(F32)
            unit = block * (lax.rsqrt(jnp.sum(block * block, axis=1, keepdims=True) + 1e-06) * scale)
            high = unit.astype(BF).astype(F32)
            AQ[g, pl.ds(base, ROWS, stride=8), :] = high
            AQ[g, pl.ds(base + 1, ROWS, stride=8), :] = unit - high
            units.append(unit)
        for spare in range(4, 8):
            AQ[g, pl.ds(spare, ROWS, stride=8), :] = jnp.zeros((ROWS, 128), F32)
        cross.append(jnp.sum(q_unit[g] * k_unit[g], axis=1, keepdims=True))

    def read_rows(i):
        for u in range(STEP):
            r = STEP * i + u
            at = pl.ds(pl.multiple_of(r * 8, 8), 8)
            for g in range(2):
                a = AQ[g, at, :].astype(BF)
                for h in (2 * g, 2 * g + 1):
                    RD[h, at, :] = dot(a, ST[r, h])

    for i in range(3):
        states[i].wait()
    pl.loop(0, 3)(read_rows)
    for via in (-1, 1, -3, 3, 5, -6):
        relay(MG, meta, via)
    for i in range(3, 6):
        states[i].wait()
    pl.loop(3, 6)(read_rows)

    gated = []
    for h in range(HEADS):
        g = h // 2
        read_q = RD[h, pl.ds(0, ROWS, stride=8), :] + RD[h, pl.ds(1, ROWS, stride=8), :]
        read_k = RD[h, pl.ds(2, ROWS, stride=8), :] + RD[h, pl.ds(3, ROWS, stride=8), :]
        arg = di_ref[:, h : h + 1] + db_ref[:, h : h + 1]
        soft = jnp.maximum(arg, 0.0) + jnp.log(1.0 + jnp.exp(-jnp.abs(arg)))
        decay = jnp.exp(-jnp.exp(dl_ref[:, h : h + 1]) * soft)
        beta = sigmoid(bi_ref[:, h : h + 1])
        cols = slice(128 * h, 128 * h + 128)
        update = beta * (v_ref[:, cols].astype(F32) - decay * read_k)
        head_out = decay * read_q + cross[g] * update
        norm = head_out * lax.rsqrt(jnp.mean(head_out * head_out, axis=1, keepdims=True) + 1e-06) * hn_ref[...]
        gate = og_ref[:, cols].astype(F32)
        gated.append((norm * (gate * sigmoid(gate))).astype(BF))
    gated = jnp.concatenate(gated, axis=1)

    moved_a = {}
    for copy, k in zip(projs, (2, 1, 3, 0)):
        copy.wait()
        AP[k] = dot(gated, OP[k])
        if k:
            moved_a[k] = remote(AP.at[k], AR.at[k - 1], at_x(k))
    for k in (2, 1, 3):
        moved_w.append(remote(dp_hbm.at[0, :, x_cols(k)], D.at[x], at_x(k)))

    for delta in RELAY:
        meta[delta].wait_recv()
    lower = (iota((ROWS, ROWS), 0) > iota((ROWS, ROWS), 1)).astype(F32).astype(BF)
    lane = iota((ROWS, 256), 1)
    lane_expert = (16 * z + 2 * (lane // 32) + (lane // 16) % 2).astype(F32)
    lane_place = (lane // 2) % 8
    lane_slot = (lane % 2).astype(F32)
    for h in range(2):

        def slots_of(j, total, h=h):
            info = MG[8 * h + j]
            match = jnp.zeros((ROWS, 256), F32)
            gates = jnp.zeros((ROWS, 256), F32)
            for k in range(TOPK):
                same = info[:, k : k + 1] == lane_expert
                match = jnp.where(same, 1.0, match)
                gates = jnp.where(same, info[:, TOPK + k : TOPK + k + 1], gates)
            earlier = dot(lower, match.astype(BF))
            here = jnp.where((earlier == lane_slot) & (lane_place == j), match, 0.0)
            none = jnp.zeros((ROWS, 256), F32)
            PTL[h, j] = jnp.concatenate([here, none], axis=0).astype(BF)
            PTR[h, j] = jnp.concatenate([none, here], axis=0).astype(BF)
            return total + jnp.sum(here * gates, axis=0, keepdims=True)

        total = lax.fori_loop(0, 8, slots_of, jnp.zeros((1, 256), F32))
        GM[:, 256 * h : 256 * h + 256] = jnp.broadcast_to(total, (8, 256))
    GS[me] = GM[...]
    moved_g = [remote(GM, GS.at[me], at_y(k)) for k in range(1, 8)]
    for h in range(2):
        PL[h] = jnp.transpose(PTL[h].reshape(8 * CH, 256).astype(F32)).astype(BF)
        PR[h] = jnp.transpose(PTR[h].reshape(8 * CH, 256).astype(F32)).astype(BF)

    for k in (1, 3, 2):
        moved_a[k].wait_recv()
    gain = pn_ref[:, x_cols(0)]
    stream = res_ref[:, x_cols(0)].astype(F32) + ((AP[0] + AR[0]) + (AR[1] + AR[2]))
    SM[...] = jnp.concatenate([stream[:, :CW], stream[:, CW:]], axis=0)
    scaled = stream * gain
    G[0] = jnp.concatenate([scaled[:, :CW], scaled[:, CW:]], axis=0).astype(BF)
    rows_z = direct(G)

    for copy in moved_g:
        copy.wait_recv()
    parts = []
    from_all = GS[:, 0, :]
    for h in range(2):
        part = jnp.zeros((8, 32), F32)
        for d in range(8):
            part = part + jnp.where(me == d, from_all[:, 256 * h + 32 * d : 256 * h + 32 * d + 32], 0.0)
        parts.append(part)
    slot_gate = jnp.concatenate(parts + [jnp.zeros((8, 64), F32)], axis=1)
    taken = (slot_gate > 0.0).astype(F32)
    taken16 = taken.astype(BF)

    def fields(dim):
        at = iota((128, 128), dim)
        nth = (at // 32) * 8 + (at // 2) % 8
        far = (nth + 1) // 2
        place = (z + jnp.where(nth % 2 == 1, -far, far) + 16) % 16
        return (at // 16) % 2, place, at % 2

    p_from, z_from, s_from = fields(0)
    p_to, z_to, s_to = fields(1)
    same_p = p_from == p_to
    before_z = (same_p & (z_from < z_to)).astype(F32).astype(BF)
    same_z = (same_p & (z_from == z_to)).astype(F32).astype(BF)
    before_s = (same_p & (z_from == z_to) & (s_from < s_to)).astype(F32).astype(BF)
    before_d = (iota((8, 8), 0) > iota((8, 8), 1)).astype(F32).astype(BF)
    ones = jnp.ones((8, 8), BF)
    rank = (
        dot(dot(ones, taken16).astype(BF), before_z)
        + dot(dot(before_d, taken16).astype(BF), same_z)
        + dot(taken16, before_s)
    )
    limit_0 = cap_ref[2 * row].astype(F32)
    limit_1 = cap_ref[2 * row + 1].astype(F32)
    limit = jnp.where((iota((8, 128), 1) // 16) % 2 == 0, limit_0, limit_1)
    kept = jnp.where(rank < limit, slot_gate, 0.0)
    kept_t = jnp.transpose(jnp.concatenate([kept] * 16, axis=0))
    for h in range(2):
        for p in range(2):
            at = (2 * h + p) * 16
            column = jnp.concatenate([kept_t[at : at + 16, d : d + 1] for d in range(8)], axis=0)
            KW[h, p] = jnp.broadcast_to(column, (128, 128))

    for via in (-1, 1, -3, 3, 5, -6):
        relay(G, rows_z, via)

    moved_y = []

    def select(h):
        for delta in ORDER[8 * h : 8 * h + 8]:
            if delta and delta not in RELAY.values():
                rows_z[delta].wait_recv()
        chunks = G[8 * h : 8 * h + 8].reshape(8 * CH, CW)
        S[h, :, :, :, 0:CW] = dot(PL[h], chunks).astype(BF).reshape(8, 2, 16, CW)
        S[h, :, :, :, CW:DX] = dot(PR[h], chunks).astype(BF).reshape(8, 2, 16, CW)
        moved_y.append([remote(S.at[h, ds[k]], R.at[h, :, me], at_y(k)) for k in range(1, 8)])
        for p in range(2):
            R[h, p, me] = S[h, me, p]

    moved_m = []

    def products(h):
        for copy in moved_y[h]:
            copy.wait_recv()
        for p in range(2):
            block = R[h, p].reshape(128, DX)
            for t in range(2):
                MS[h, 2 * p + t] = dot(block, W[2 * p + t]).astype(BF)
            plain = block.astype(F32) / gain
            squares = jnp.sum(plain * plain, axis=1, keepdims=True)
            SSB[h, p] = jnp.transpose(jnp.broadcast_to(squares, (128, 128)))[0:8]
        moved = []
        for k in (2, 1, 3):
            moved.append(remote(MS.at[h, xs[k]], MR.at[h, k - 1], at_x(k)))
            moved.append(remote(SSB.at[h, xs[k] // 2], SSR.at[h, k - 1], at_x(k)))
        moved_m.append(moved)

    moved_i = []

    def activate(h):
        for copy in moved_m[h]:
            copy.wait_recv()
        both = (MS[h, x].astype(F32) + MR[h, 0].astype(F32)) + (MR[h, 1].astype(F32) + MR[h, 2].astype(F32))
        squares = (SSB[h, x // 2] + SSR[h, 0]) + (SSR[h, 1] + SSR[h, 2])
        squares = jnp.transpose(jnp.concatenate([squares] * 16, axis=0))[:, 0:1]
        scale = lax.rsqrt(squares * (1.0 / 2048.0) + 1e-06)
        gate = both[:, 0:128] * scale
        up = both[:, 128:256] * scale
        IN[h, x] = (gate * sigmoid(gate) * up).astype(BF)
        moved_i.append([remote(IN.at[h, x], IN.at[h, x], at_x(k)) for k in (2, 1, 3)])

    moved_r = []

    def down(h):
        for copy in moved_i[h]:
            copy.wait_recv()
        for p in range(2):
            inner = jnp.concatenate([IN[h, 2 * p], IN[h, 2 * p + 1]], axis=1)
            part = dot(inner, D[2 * p : 2 * p + 2].reshape(256, DX))
            weight = KW[h, p]
            part = part * jnp.concatenate([weight] * 4, axis=1)
            Y[h, :, p] = part.astype(BF).reshape(8, 16, DX)
        moved_r.append([remote(Y.at[h, ds[k]], R2.at[h, me], at_y(k)) for k in range(1, 8)])
        R2[h, me] = Y[h, me]

    def combine(h):
        for copy in moved_r[h]:
            copy.wait_recv()
        back = R2[h].reshape(256, DX)
        left = dot(PTL[h].reshape(8 * CH, 256), back[:, 0:CW])
        right = dot(PTR[h].reshape(8 * CH, 256), back[:, CW:DX])
        C[8 * h : 8 * h + 8] = (left + right).reshape(8, CH, CW)

    select(0)
    select(1)
    for copy in own_w:
        copy.wait()
    for copy in moved_w:
        copy.wait_recv()
    products(0)
    products(1)
    activate(0)
    activate(1)
    down(0)
    down(1)
    combine(0)
    combine(1)

    back_z = {}

    def give(delta, via):
        place = PLACE[delta]
        back_z[delta] = remote(CB.at[place], T.at[place], at_z(delta - via))

    for delta, via in RELAY.items():
        CB[PLACE[delta]] = C[PLACE[delta]].astype(BF)
    for delta in (-8, -7, 7, 6, -5, -4, 4, -2, 2):
        give(delta, RELAY[delta])
    for via in (-1, 1, 3, -3, 5, -6):
        total = C[PLACE[via]]
        for delta, v in RELAY.items():
            if v == via:
                back_z[delta].wait_recv()
                total = total + T[PLACE[delta]].astype(F32)
        CB[PLACE[via]] = total.astype(BF)
        give(via, 0)
    mixed = SM[...] + C[0]
    for via in (-1, 1, 3, -3, 5, -6):
        back_z[via].wait_recv()
        mixed = mixed + T[PLACE[via]].astype(F32)

    mixed = jnp.concatenate([mixed[0:ROWS], mixed[ROWS:CH]], axis=1)
    for k in range(4):
        FX[k] = jnp.concatenate([mixed[6 * k : 6 * k + 6], jnp.zeros((2, DX), F32)], axis=0)
    FO[x] = FX[x]
    last = [remote(FX.at[xs[k]], FO.at[x], at_x(k)) for k in (2, 1, 3)]
    for copy in last:
        copy.wait_recv()
    for k in range(4):
        out_ref[:, DX * k : DX * k + DX] = FO[k, 0:6].astype(BF)
    for copy in sent:
        copy.wait_send()


def on_device(
    residual, queries, keys, values, out_gate, decay_input, beta_input, decay_log, decay_bias, past_state,
    head_norm, out_proj, post_norm, expert_ids, expert_gates, capacity, gate_proj, up_proj, down_proj,
):
    vmem = pl.BlockSpec(memory_space=pltpu.VMEM)
    smem = pl.BlockSpec(memory_space=pltpu.SMEM)
    hbm = pl.BlockSpec(memory_space=pl.ANY)
    scratch = [
        pltpu.VMEM((ROWS, HEADS, 128, 128), BF),
        pltpu.VMEM((4, DX, DX), BF),
        pltpu.VMEM((4, DX, 256), BF),
        pltpu.VMEM((4, 128, DX), BF),
        pltpu.VMEM((16, ROWS, 128), F32),
        pltpu.VMEM((2, 8 * ROWS, 128), F32),
        pltpu.VMEM((HEADS, 8 * ROWS, 128), F32),
        pltpu.VMEM((4, ROWS, DX), F32),
        pltpu.VMEM((3, ROWS, DX), F32),
        pltpu.VMEM((CH, CW), F32),
        pltpu.VMEM((16, CH, CW), BF),
        pltpu.VMEM((2, 8, CH, 256), BF),
        pltpu.VMEM((2, 8, CH, 256), BF),
        pltpu.VMEM((2, 256, 8 * CH), BF),
        pltpu.VMEM((2, 256, 8 * CH), BF),
        pltpu.VMEM((2, 8, 2, 16, DX), BF),
        pltpu.VMEM((2, 2, 8, 16, DX), BF),
        pltpu.VMEM((8, 512), F32),
        pltpu.VMEM((8, 8, 512), F32),
        pltpu.VMEM((2, 2, 128, 128), F32),
        pltpu.VMEM((2, 4, 128, 256), BF),
        pltpu.VMEM((2, 3, 128, 256), BF),
        pltpu.VMEM((2, 2, 8, 128), F32),
        pltpu.VMEM((2, 3, 8, 128), F32),
        pltpu.VMEM((2, 4, 128, 128), BF),
        pltpu.VMEM((2, 8, 2, 16, DX), BF),
        pltpu.VMEM((2, 8, 2, 16, DX), BF),
        pltpu.VMEM((16, CH, CW), F32),
        pltpu.VMEM((16, CH, CW), BF),
        pltpu.VMEM((16, CH, CW), BF),
        pltpu.VMEM((4, 8, DX), F32),
        pltpu.VMEM((4, 8, DX), F32),
        pltpu.SemaphoreType.DMA((N_SEM,)),
        pltpu.SemaphoreType.DMA((N_SEM,)),
        pltpu.SemaphoreType.DMA((16,)),
    ]
    return pl.pallas_call(
        kernel,
        out_shape=jax.ShapeDtypeStruct((6, 2048), BF),
        in_specs=[vmem] * 13 + [smem] + [hbm] * 5,
        out_specs=vmem,
        scratch_shapes=scratch,
        compiler_params=pltpu.CompilerParams(
            collective_id=1, has_side_effects=True, vmem_limit_bytes=40 * 1024 * 1024
        ),
        name="layer",
    )(
        residual, queries, keys, values, out_gate, decay_input, beta_input, decay_log[None, :], decay_bias[None, :],
        head_norm[None, :], post_norm[None, :], expert_ids, expert_gates, capacity,
        past_state, out_proj, gate_proj, up_proj, down_proj,
    )


def solution(mesh):
    placed = (
        P("row", None),
        P("row", "head"),
        P("row", "head"),
        P("row", "head"),
        P("row", "head"),
        P("row", "head"),
        P("row", "head"),
        P("head"),
        P("head"),
        P("row", "head", None, None),
        P(),
        P("head", None),
        P(),
        P("row", None),
        P("row", None),
        P(),
        P("row", None, "head"),
        P("row", None, "head"),
        P("row", "head", None),
    )
    return jax.shard_map(
        on_device, mesh=mesh, in_specs=placed, out_specs=P(("row", "head"), None), check_vma=False
    )
```

time: 290 us -> 105 us (0.36)
  the two profiles are of different devices: /device:TPU:6 before, /device:TPU:64 now
where the time goes in v1:
time: 105 us; the launch traced here: 104 us
  Pallas kernels  86.7 us (83%)
  local copies, waits for them, and re-layouts  17.4 us (17%)
    pallas_call x1, Pallas kernels, on_device(): pl.pallas_call(kernel, out_shape=jax.ShapeDtypeStruct((6, 2048), BF), in_...  86.7 us
    unnamed x35, local copies, waits for them, and re-layouts  17.4 us

profile of v1, /device:TPU:64, one launch (start us, length us, event | category | flops | bytes accessed | tf_op | source)
XLA Modules:
  0.0 104.2 jit_solution(8354116357124100993)
XLA Ops:
  0.0 0.8 copy.20.di_ref
  0.8 0.8 copy.21.bi_ref
  1.5 0.8 copy.22.ids_ref
  2.3 0.8 copy.23.eg_ref
  3.1 0.0 copy-start
  3.1 1.9 %copy-done = bf16[24,4,128,128]{3,2,1,0:T(8,128)(2,1)S(1)} copy-done((bf16[24,4,128,128]{3,2,1,0:T(8,128)(2,1)S(1)}, bf16[24,4,128,128]{3,2,1,0:T(8,128)(2,1)}, u32[]{:S(2)}) %copy-start) | copy-done | bytes 3145752
  5.0 0.0 copy-start.1
  5.0 1.6 %copy-done.1 = bf16[512,2048]{1,0:T(8,128)(2,1)S(1)} copy-done((bf16[512,2048]{1,0:T(8,128)(2,1)S(1)}, bf16[512,2048]{1,0:T(8,128)(2,1)}, u32[]{:S(2)}) %copy-start.1) | copy-done | bytes 2097176
  6.5 0.0 copy-start.2
  6.6 1.0 copy-done.2
  7.6 0.0 copy-start.3
  7.6 1.0 copy-done.3
  8.6 0.0 copy-start.4
  8.6 1.0 copy-done.4
  9.7 0.0 copy-start.5
  9.7 0.9 copy-done.5
  10.6 0.0 copy-start.6
  10.6 0.7 copy-done.6
  11.3 0.0 copy-start.7
  11.3 0.7 copy-done.7
  12.0 0.0 copy-start.8
  12.0 0.7 copy-done.8
  12.8 0.0 copy-start.9
  12.8 0.7 copy-done.9
  13.5 0.0 copy-start.10
  13.5 0.7 copy-done.10
  14.2 0.0 copy-start.11
  14.2 0.7 copy-done.11
  14.8 0.0 copy-start.12
  14.8 0.7 copy-done.12
  15.5 0.0 copy-start.13
  15.5 0.7 copy-done.13
  16.1 0.0 copy-start.14
  16.1 0.7 copy-done.14
  16.8 86.7 %layer.1 = bf16[6,2048]{1,0:T(8,128)(2,1)S(1)} custom-call(bf16[24,2048]{1,0:T(8,128)(2,1)S(1)} %copy-done.5, bf16[24,256]{1,0:T(8,128)(2,1)S(1)} %copy-done.8, bf16[24,256]{1,0:T(8,128)(2,1)S(1)} %copy-done.9, bf16[24,512]{1,0:T(8,128)(2,1)S(1)} %copy-done.6, bf16[24,512]{1,0:T(8,128)(2,1)S(1)} %copy-done.7, f32[24,4]{1,0:T(8,128)S(1)} %copy.20.di_ref, ...), custom_call_target="tpu_custom_call" | custom-call | tf_op jit(solution)/shard_map/layer/pallas_call | solution.py:424
  103.5 0.6 copy.25
Async XLA Ops:
  3.1 1.9 %copy-start = (bf16[24,4,128,128]{3,2,1,0:T(8,128)(2,1)S(1)}, bf16[24,4,128,128]{3,2,1,0:T(8,128)(2,1)}, u32[]{:S(2)}) copy-start(bf16[24,4,128,128]{3,2,1,0:T(8,128)(2,1)} %state_hbm.1) | copy-start | bytes 9437188
  5.0 1.6 %copy-start.1 = (bf16[512,2048]{1,0:T(8,128)(2,1)S(1)}, bf16[512,2048]{1,0:T(8,128)(2,1)}, u32[]{:S(2)}) copy-start(bf16[512,2048]{1,0:T(8,128)(2,1)} %op_hbm.1) | copy-start | bytes 6291460
  6.5 1.0 %copy-start.2 = (bf16[1,2048,128]{2,1,0:T(8,128)(2,1)S(1)}, bf16[1,2048,128]{2,1,0:T(8,128)(2,1)}, u32[]{:S(2)}) copy-start(bf16[1,2048,128]{2,1,0:T(8,128)(2,1)} %gp_hbm.1) | copy-start | bytes 1572868
  7.6 1.0 %copy-start.3 = (bf16[1,2048,128]{2,1,0:T(8,128)(2,1)S(1)}, bf16[1,2048,128]{2,1,0:T(8,128)(2,1)}, u32[]{:S(2)}) copy-start(bf16[1,2048,128]{2,1,0:T(8,128)(2,1)} %up_hbm.1) | copy-start | bytes 1572868
  8.6 1.0 %copy-start.4 = (bf16[1,128,2048]{2,1,0:T(8,128)(2,1)S(1)}, bf16[1,128,2048]{2,1,0:T(8,128)(2,1)}, u32[]{:S(2)}) copy-start(bf16[1,128,2048]{2,1,0:T(8,128)(2,1)} %dp_hbm.1) | copy-start | bytes 1572868
  9.7 0.9 copy-start.5
  10.6 0.7 copy-start.6
  11.3 0.7 copy-start.7
  12.0 0.7 copy-start.8
  12.8 0.7 copy-start.9
  13.5 0.7 copy-start.10
  14.2 0.7 copy-start.11
  14.8 0.7 copy-start.12
  15.5 0.7 copy-start.13
  16.1 0.7 copy-start.14

commit v2 on v1

--- a/solution.py
+++ b/solution.py
@@ -22,7 +22,9 @@
 DIRECT = (-6, 5, -3, 3, -1, 1)
 RELAY = {-2: -1, 2: 1, -4: -3, -5: -3, 4: 3, 6: 5, 7: 5, -7: -6, -8: -6}
 REACH = (-6, -5, -3, -2, -1, 1, 2, 3, 5, 6)
+LEAVES = ((-4, -2, 2), (-8, -7, 7, 6, -5, 4))
 N_SEM = 128
+GATE_AT, DECAY_AT, BETA_AT = 16, 32, 40
 
 
 def dot(a, b):
@@ -38,10 +40,12 @@
 
 
 def kernel(
-    res_ref, q_ref, k_ref, v_ref, og_ref, di_ref, bi_ref, dl_ref, db_ref, hn_ref, pn_ref,
-    ids_ref, eg_ref, cap_ref, state_hbm, op_hbm, gp_hbm, up_hbm, dp_hbm,
+    res_hbm, q_hbm, k_hbm, v_hbm, og_hbm, di_hbm, bi_hbm, dl_hbm, db_hbm, hn_hbm, pn_hbm,
+    ids_hbm, eg_hbm, cap_hbm, state_hbm, op_hbm, gp_hbm, up_hbm, dp_hbm,
     out_ref,
-    ST, OP, W, D, MG, AQ, RD, AP, AR, SM, G, PTL, PTR, PL, PR, S, R, GM, GS, KW,
+    res_ref, q_ref, k_ref, v_ref, og_ref, di_ref, bi_ref, dl_ref, db_ref, hn_ref, pn_ref, ids_ref, eg_ref, cap_ref,
+    NT,
+    ST, OP, W, D, MG, AQ, RD, AP, AR, SM, G, PTL, PTR, PL, PR, S, R, MT, GT, GM, GS, KW,
     MS, MR, SSB, SSR, IN, Y, R2, C, CB, T, FX, FO,
     ss, rs, ls,
 ):
@@ -83,7 +87,21 @@
     def x_cols(k):
         return pl.ds(pl.multiple_of(xs[k] * DX, DX), DX)
 
+    barrier = pltpu.get_barrier_semaphore()
+    peers = [at_z(off) for off in REACH] + [at_y(k) for k in range(1, 8)] + [at_x(k) for k in range(1, 4)]
+    for device in peers:
+        pl.semaphore_signal(barrier, inc=1, device_id=device, device_id_type=MESH)
+
+    lists = [local(ids_hbm, ids_ref), local(eg_hbm, eg_ref), local(di_hbm, di_ref), local(bi_hbm, bi_ref)]
+    heads = [
+        local(a, b)
+        for a, b in (
+            (q_hbm, q_ref), (k_hbm, k_ref), (v_hbm, v_ref), (og_hbm, og_ref), (dl_hbm, dl_ref), (db_hbm, db_ref),
+            (hn_hbm, hn_ref),
+        )
+    ]
     states = [local(state_hbm.at[pl.ds(STEP * i, STEP)], ST.at[pl.ds(STEP * i, STEP)]) for i in range(ROWS // STEP)]
+    later = [local(cap_hbm, cap_ref), local(res_hbm.at[:, x_cols(0)], res_ref), local(pn_hbm.at[:, x_cols(0)], pn_ref)]
     projs = [local(op_hbm.at[:, x_cols(k)], OP.at[k]) for k in (2, 1, 3, 0)]
     own_w = [
         local(gp_hbm.at[0, x_cols(0), :], W.at[x, :, pl.ds(0, 128)]),
@@ -91,10 +109,14 @@
         local(dp_hbm.at[0, :, x_cols(0)], D.at[x]),
     ]
 
-    barrier = pltpu.get_barrier_semaphore()
-    peers = [at_z(off) for off in REACH] + [at_y(k) for k in range(1, 8)] + [at_x(k) for k in range(1, 4)]
-    for device in peers:
-        pl.semaphore_signal(barrier, inc=1, device_id=device, device_id_type=MESH)
+    for copy in lists:
+        copy.wait()
+    NT[...] = jnp.zeros((128, 128), F32)
+    NT[0:TOPK, 0:ROWS] = ids_ref[...].astype(F32)
+    NT[GATE_AT : GATE_AT + TOPK, 0:ROWS] = eg_ref[...]
+    NT[DECAY_AT : DECAY_AT + HEADS, 0:ROWS] = di_ref[...]
+    NT[BETA_AT : BETA_AT + HEADS, 0:ROWS] = bi_ref[...]
+    MG[0] = jnp.transpose(NT[...])[0:ROWS]
     pl.semaphore_wait(barrier, len(peers))
 
     def direct(buf):
@@ -106,14 +128,13 @@
             if v == via:
                 copies[delta] = remote(buf.at[PLACE[v]], buf.at[PLACE[delta]], at_z(v - delta))
 
-    MG[0] = jnp.concatenate([ids_ref[...].astype(F32), eg_ref[...], jnp.zeros((ROWS, 128 - 2 * TOPK), F32)], axis=1)
     meta = direct(MG)
 
-    moved_w = []
-    for k in (2, 1, 3):
-        moved_w.append(remote(gp_hbm.at[0, x_cols(k), :], W.at[x, :, pl.ds(0, 128)], at_x(k)))
-        moved_w.append(remote(up_hbm.at[0, x_cols(k), :], W.at[x, :, pl.ds(128, 128)], at_x(k)))
-
+    moved_w = [remote(gp_hbm.at[0, x_cols(k), :], W.at[x, :, pl.ds(0, 128)], at_x(k)) for k in (1, 3)]
+
+    for copy in heads:
+        copy.wait()
+    narrow = MG[0]
     q_unit, k_unit, cross = [], [], []
     for g in range(2):
         for ref, scale, units, base in ((q_ref, 128 ** (-0.5), q_unit, 0), (k_ref, 1.0, k_unit, 2)):
@@ -136,24 +157,19 @@
                 for h in (2 * g, 2 * g + 1):
                     RD[h, at, :] = dot(a, ST[r, h])
 
-    for i in range(3):
-        states[i].wait()
-    pl.loop(0, 3)(read_rows)
-    for via in (-1, 1, -3, 3, 5, -6):
-        relay(MG, meta, via)
-    for i in range(3, 6):
-        states[i].wait()
-    pl.loop(3, 6)(read_rows)
+    for copy in states:
+        copy.wait()
+    pl.loop(0, ROWS // STEP)(read_rows)
 
     gated = []
     for h in range(HEADS):
         g = h // 2
         read_q = RD[h, pl.ds(0, ROWS, stride=8), :] + RD[h, pl.ds(1, ROWS, stride=8), :]
         read_k = RD[h, pl.ds(2, ROWS, stride=8), :] + RD[h, pl.ds(3, ROWS, stride=8), :]
-        arg = di_ref[:, h : h + 1] + db_ref[:, h : h + 1]
+        arg = narrow[:, DECAY_AT + h : DECAY_AT + h + 1] + db_ref[:, h : h + 1]
         soft = jnp.maximum(arg, 0.0) + jnp.log(1.0 + jnp.exp(-jnp.abs(arg)))
         decay = jnp.exp(-jnp.exp(dl_ref[:, h : h + 1]) * soft)
-        beta = sigmoid(bi_ref[:, h : h + 1])
+        beta = sigmoid(narrow[:, BETA_AT + h : BETA_AT + h + 1])
         cols = slice(128 * h, 128 * h + 128)
         update = beta * (v_ref[:, cols].astype(F32) - decay * read_k)
         head_out = decay * read_q + cross[g] * update
@@ -168,96 +184,74 @@
         AP[k] = dot(gated, OP[k])
         if k:
             moved_a[k] = remote(AP.at[k], AR.at[k - 1], at_x(k))
-    for k in (2, 1, 3):
-        moved_w.append(remote(dp_hbm.at[0, :, x_cols(k)], D.at[x], at_x(k)))
-
-    for delta in RELAY:
-        meta[delta].wait_recv()
-    lower = (iota((ROWS, ROWS), 0) > iota((ROWS, ROWS), 1)).astype(F32).astype(BF)
-    lane = iota((ROWS, 256), 1)
-    lane_expert = (16 * z + 2 * (lane // 32) + (lane // 16) % 2).astype(F32)
-    lane_place = (lane // 2) % 8
-    lane_slot = (lane % 2).astype(F32)
-    for h in range(2):
-
-        def slots_of(j, total, h=h):
-            info = MG[8 * h + j]
-            match = jnp.zeros((ROWS, 256), F32)
-            gates = jnp.zeros((ROWS, 256), F32)
-            for k in range(TOPK):
-                same = info[:, k : k + 1] == lane_expert
-                match = jnp.where(same, 1.0, match)
-                gates = jnp.where(same, info[:, TOPK + k : TOPK + k + 1], gates)
-            earlier = dot(lower, match.astype(BF))
-            here = jnp.where((earlier == lane_slot) & (lane_place == j), match, 0.0)
-            none = jnp.zeros((ROWS, 256), F32)
-            PTL[h, j] = jnp.concatenate([here, none], axis=0).astype(BF)
-            PTR[h, j] = jnp.concatenate([none, here], axis=0).astype(BF)
-            return total + jnp.sum(here * gates, axis=0, keepdims=True)
-
-        total = lax.fori_loop(0, 8, slots_of, jnp.zeros((1, 256), F32))
-        GM[:, 256 * h : 256 * h + 256] = jnp.broadcast_to(total, (8, 256))
-    GS[me] = GM[...]
-    moved_g = [remote(GM, GS.at[me], at_y(k)) for k in range(1, 8)]
-    for h in range(2):
-        PL[h] = jnp.transpose(PTL[h].reshape(8 * CH, 256).astype(F32)).astype(BF)
-        PR[h] = jnp.transpose(PTR[h].reshape(8 * CH, 256).astype(F32)).astype(BF)
+
+    for via in (-1, 1, -3, 3):
+        relay(MG, meta, via)
 
     for k in (1, 3, 2):
         moved_a[k].wait_recv()
-    gain = pn_ref[:, x_cols(0)]
-    stream = res_ref[:, x_cols(0)].astype(F32) + ((AP[0] + AR[0]) + (AR[1] + AR[2]))
+    for copy in later:
+        copy.wait()
+    gain = pn_ref[...]
+    inverse = 1.0 / gain
+    stream = res_ref[...].astype(F32) + ((AP[0] + AR[0]) + (AR[1] + AR[2]))
     SM[...] = jnp.concatenate([stream[:, :CW], stream[:, CW:]], axis=0)
     scaled = stream * gain
     G[0] = jnp.concatenate([scaled[:, :CW], scaled[:, CW:]], axis=0).astype(BF)
     rows_z = direct(G)
-
-    for copy in moved_g:
-        copy.wait_recv()
-    parts = []
-    from_all = GS[:, 0, :]
-    for h in range(2):
-        part = jnp.zeros((8, 32), F32)
-        for d in range(8):
-            part = part + jnp.where(me == d, from_all[:, 256 * h + 32 * d : 256 * h + 32 * d + 32], 0.0)
-        parts.append(part)
-    slot_gate = jnp.concatenate(parts + [jnp.zeros((8, 64), F32)], axis=1)
-    taken = (slot_gate > 0.0).astype(F32)
-    taken16 = taken.astype(BF)
-
-    def fields(dim):
-        at = iota((128, 128), dim)
-        nth = (at // 32) * 8 + (at // 2) % 8
-        far = (nth + 1) // 2
-        place = (z + jnp.where(nth % 2 == 1, -far, far) + 16) % 16
-        return (at // 16) % 2, place, at % 2
-
-    p_from, z_from, s_from = fields(0)
-    p_to, z_to, s_to = fields(1)
-    same_p = p_from == p_to
-    before_z = (same_p & (z_from < z_to)).astype(F32).astype(BF)
-    same_z = (same_p & (z_from == z_to)).astype(F32).astype(BF)
-    before_s = (same_p & (z_from == z_to) & (s_from < s_to)).astype(F32).astype(BF)
-    before_d = (iota((8, 8), 0) > iota((8, 8), 1)).astype(F32).astype(BF)
-    ones = jnp.ones((8, 8), BF)
-    rank = (
-        dot(dot(ones, taken16).astype(BF), before_z)
-        + dot(dot(before_d, taken16).astype(BF), same_z)
-        + dot(taken16, before_s)
+    moved_w.append(remote(gp_hbm.at[0, x_cols(2), :], W.at[x, :, pl.ds(0, 128)], at_x(2)))
+    for k in (2, 1, 3):
+        moved_w.append(remote(up_hbm.at[0, x_cols(k), :], W.at[x, :, pl.ds(128, 128)], at_x(k)))
+    moved_d = [remote(dp_hbm.at[0, :, x_cols(k)], D.at[x], at_x(k)) for k in (2, 1, 3)]
+
+    for via in (5, -6):
+        relay(MG, meta, via)
+    for delta in RELAY:
+        meta[delta].wait_recv()
+    lane = iota((ROWS, 128), 1)
+    lane_expert = jnp.where(lane < 32, 16 * z + lane // 2, -1).astype(F32)
+
+    def name_slots(i):
+        for u in range(4):
+            j = 4 * i + u
+            info = MG[j]
+            match = jnp.zeros((ROWS, 128), F32)
+            gates = jnp.zeros((ROWS, 128), F32)
+            for k in range(TOPK):
+                same = info[:, k : k + 1] == lane_expert
+                match = jnp.where(same, 1.0, match)
+                gates = jnp.where(same, info[:, GATE_AT + k : GATE_AT + k + 1], gates)
+            at = pl.ds(pl.multiple_of(j * ROWS, 8), ROWS)
+            MT[at, :] = match
+            GT[at, :] = gates
+
+    pl.loop(0, 4)(name_slots)
+    half = 8 * ROWS
+    row_a, row_b = iota((half, half), 0), iota((half, half), 1)
+    lower = ((row_a > row_b) & (row_a // ROWS == row_b // ROWS)).astype(F32).astype(BF)
+    spread = (
+        (iota((128, 256), 0) // 2 == iota((128, 256), 1) // 16)
+        & (iota((128, 256), 0) % 2 == (iota((128, 256), 1) // 8) % 2)
     )
-    limit_0 = cap_ref[2 * row].astype(F32)
-    limit_1 = cap_ref[2 * row + 1].astype(F32)
-    limit = jnp.where((iota((8, 128), 1) // 16) % 2 == 0, limit_0, limit_1)
-    kept = jnp.where(rank < limit, slot_gate, 0.0)
-    kept_t = jnp.transpose(jnp.concatenate([kept] * 16, axis=0))
-    for h in range(2):
-        for p in range(2):
-            at = (2 * h + p) * 16
-            column = jnp.concatenate([kept_t[at : at + 16, d : d + 1] for d in range(8)], axis=0)
-            KW[h, p] = jnp.broadcast_to(column, (128, 128))
-
-    for via in (-1, 1, -3, 3, 5, -6):
-        relay(G, rows_z, via)
+    spread = spread.astype(F32).astype(BF)
+    lane_slot = (iota((half, 128), 1) % 2).astype(F32)
+    lane_place = iota((half, 256), 1) % 8
+    def place_slots(h):
+        match = MT[half * h : half * h + half, :]
+        earlier = dot(lower, match.astype(BF))
+        here = jnp.where(earlier == lane_slot, match, 0.0)
+        gates = here * GT[half * h : half * h + half, :]
+        GM[8 * h : 8 * h + 8, :] = jnp.concatenate(
+            [jnp.sum(gates[ROWS * j : ROWS * j + ROWS], axis=0, keepdims=True) for j in range(8)], axis=0
+        )
+        placed = jnp.where(lane_place == iota((half, 256), 0) // ROWS, dot(here.astype(BF), spread), 0.0)
+        none = jnp.zeros((ROWS, 256), F32)
+        for j in range(8):
+            one = placed[ROWS * j : ROWS * j + ROWS]
+            PTL[h, j] = jnp.concatenate([one, none], axis=0).astype(BF)
+            PTR[h, j] = jnp.concatenate([none, one], axis=0).astype(BF)
+        PL[h] = jnp.transpose(PTL[h].reshape(8 * CH, 256).astype(F32)).astype(BF)
+        PR[h] = jnp.transpose(PTR[h].reshape(8 * CH, 256).astype(F32)).astype(BF)
 
     moved_y = []
 
@@ -281,7 +275,7 @@
             block = R[h, p].reshape(128, DX)
             for t in range(2):
                 MS[h, 2 * p + t] = dot(block, W[2 * p + t]).astype(BF)
-            plain = block.astype(F32) / gain
+            plain = block.astype(F32) * inverse
             squares = jnp.sum(plain * plain, axis=1, keepdims=True)
             SSB[h, p] = jnp.transpose(jnp.broadcast_to(squares, (128, 128)))[0:8]
         moved = []
@@ -307,6 +301,9 @@
     moved_r = []
 
     def down(h):
+        if h == 0:
+            for copy in moved_d:
+                copy.wait_recv()
         for copy in moved_i[h]:
             copy.wait_recv()
         for p in range(2):
@@ -326,8 +323,60 @@
         right = dot(PTR[h].reshape(8 * CH, 256), back[:, CW:DX])
         C[8 * h : 8 * h + 8] = (left + right).reshape(8, CH, CW)
 
+    back_z = {}
+
+    def give(delta, via):
+        place = PLACE[delta]
+        back_z[delta] = remote(CB.at[place], T.at[place], at_z(delta - via))
+
+    def leaves(h):
+        for delta in LEAVES[h]:
+            CB[PLACE[delta]] = C[PLACE[delta]].astype(BF)
+            give(delta, RELAY[delta])
+
+    def weigh():
+        for copy in moved_g:
+            copy.wait_recv()
+        slot_gate = GS[...].reshape(128, 128)
+        taken = (slot_gate > 0.0).astype(F32).astype(BF)
+
+        def order(dim):
+            at = iota((128, 128), dim)
+            nth = at % 16
+            far = (nth + 1) // 2
+            place = (z + jnp.where(nth % 2 == 1, -far, far) + 16) % 16
+            return place * 8 + at // 16
+
+        before = (order(1) < order(0)).astype(F32).astype(BF)
+        lane_a, lane_b = iota((128, 128), 0), iota((128, 128), 1)
+        pair = (lane_a // 2 == lane_b // 2).astype(F32).astype(BF)
+        first = ((lane_a // 2 == lane_b // 2) & (lane_a < lane_b)).astype(F32).astype(BF)
+        rank = dot(before, dot(taken, pair).astype(BF)) + dot(taken, first)
+        limit_0 = cap_ref[2 * row].astype(F32)
+        limit_1 = cap_ref[2 * row + 1].astype(F32)
+        limit = jnp.where((lane_b // 2) % 2 == 0, limit_0, limit_1)
+        kept = jnp.where(rank < limit, slot_gate, 0.0)
+        for p in range(2):
+            columns = [
+                jnp.sum(jnp.where(lane_b == 4 * me + 2 * p + t, kept, 0.0), axis=1, keepdims=True) for t in range(2)
+            ]
+            for h in range(2):
+                column = jnp.concatenate(
+                    [c[16 * d + 8 * h : 16 * d + 8 * h + 8] for d in range(8) for c in columns], axis=0
+                )
+                KW[h, p] = jnp.broadcast_to(column, (128, 128))
+
+    for via in (-1, 1, -3, 3):
+        relay(G, rows_z, via)
+    place_slots(0)
+    for via in (5, -6):
+        relay(G, rows_z, via)
     select(0)
+    place_slots(1)
     select(1)
+    GS[me] = GM[...]
+    moved_g = [remote(GM, GS.at[me], at_y(k)) for k in range(1, 8)]
+
     for copy in own_w:
         copy.wait()
     for copy in moved_w:
@@ -335,23 +384,16 @@
     products(0)
     products(1)
     activate(0)
+    weigh()
     activate(1)
     down(0)
     down(1)
     combine(0)
+    leaves(0)
     combine(1)
-
-    back_z = {}
-
-    def give(delta, via):
-        place = PLACE[delta]
-        back_z[delta] = remote(CB.at[place], T.at[place], at_z(delta - via))
-
-    for delta, via in RELAY.items():
-        CB[PLACE[delta]] = C[PLACE[delta]].astype(BF)
-    for delta in (-8, -7, 7, 6, -5, -4, 4, -2, 2):
-        give(delta, RELAY[delta])
-    for via in (-1, 1, 3, -3, 5, -6):
+    leaves(1)
+
+    for via in (-6, 5, -3, 3, -1, 1):
         total = C[PLACE[via]]
         for delta, v in RELAY.items():
             if v == via:
@@ -382,9 +424,23 @@
     head_norm, out_proj, post_norm, expert_ids, expert_gates, capacity, gate_proj, up_proj, down_proj,
 ):
     vmem = pl.BlockSpec(memory_space=pltpu.VMEM)
-    smem = pl.BlockSpec(memory_space=pltpu.SMEM)
     hbm = pl.BlockSpec(memory_space=pl.ANY)
     scratch = [
+        pltpu.VMEM((ROWS, DX), BF),
+        pltpu.VMEM((ROWS, 256), BF),
+        pltpu.VMEM((ROWS, 256), BF),
+        pltpu.VMEM((ROWS, DX), BF),
+        pltpu.VMEM((ROWS, DX), BF),
+        pltpu.VMEM((HEADS, ROWS), F32),
+        pltpu.VMEM((HEADS, ROWS), F32),
+        pltpu.VMEM((1, HEADS), F32),
+        pltpu.VMEM((1, HEADS), F32),
+        pltpu.VMEM((1, 128), F32),
+        pltpu.VMEM((1, DX), F32),
+        pltpu.VMEM((TOPK, ROWS), jnp.int32),
+        pltpu.VMEM((TOPK, ROWS), F32),
+        pltpu.SMEM((256,), jnp.int32),
+        pltpu.VMEM((128, 128), F32),
         pltpu.VMEM((ROWS, HEADS, 128, 128), BF),
         pltpu.VMEM((4, DX, DX), BF),
         pltpu.VMEM((4, DX, 256), BF),
@@ -402,8 +458,10 @@
         pltpu.VMEM((2, 256, 8 * CH), BF),
         pltpu.VMEM((2, 8, 2, 16, DX), BF),
         pltpu.VMEM((2, 2, 8, 16, DX), BF),
-        pltpu.VMEM((8, 512), F32),
-        pltpu.VMEM((8, 8, 512), F32),
+        pltpu.VMEM((16 * ROWS, 128), F32),
+        pltpu.VMEM((16 * ROWS, 128), F32),
+        pltpu.VMEM((16, 128), F32),
+        pltpu.VMEM((8, 16, 128), F32),
         pltpu.VMEM((2, 2, 128, 128), F32),
         pltpu.VMEM((2, 4, 128, 256), BF),
         pltpu.VMEM((2, 3, 128, 256), BF),
@@ -419,22 +477,24 @@
         pltpu.VMEM((4, 8, DX), F32),
         pltpu.SemaphoreType.DMA((N_SEM,)),
         pltpu.SemaphoreType.DMA((N_SEM,)),
-        pltpu.SemaphoreType.DMA((16,)),
+        pltpu.SemaphoreType.DMA((32,)),
     ]
     return pl.pallas_call(
         kernel,
-        out_shape=jax.ShapeDtypeStruct((6, 2048), BF),
-        in_specs=[vmem] * 13 + [smem] + [hbm] * 5,
+        out_shape=pltpu.VMEM((6, 2048), BF),
+        in_specs=[hbm] * 19,
         out_specs=vmem,
         scratch_shapes=scratch,
         compiler_params=pltpu.CompilerParams(
-            collective_id=1, has_side_effects=True, vmem_limit_bytes=40 * 1024 * 1024
+            collective_id=1, has_side_effects=True, vmem_limit_bytes=60 * 1024 * 1024
         ),
         name="layer",
     )(
-        residual, queries, keys, values, out_gate, decay_input, beta_input, decay_log[None, :], decay_bias[None, :],
-        head_norm[None, :], post_norm[None, :], expert_ids, expert_gates, capacity,
+        *[pltpu.with_memory_space_constraint(array, pltpu.HBM) for array in (
+        residual, queries, keys, values, out_gate, decay_input.T, beta_input.T, decay_log[None, :], decay_bias[None, :],
+        head_norm[None, :], post_norm[None, :], expert_ids.T, expert_gates.T, capacity,
         past_state, out_proj, gate_proj, up_proj, down_proj,
+        )]
     )
 
 

time: 105 us -> 78.3 us (0.75)
  the two profiles are of different devices: /device:TPU:64 before, /device:TPU:6 now
where the time goes in v2:
time: 78.3 us; the launch traced here: 77.7 us
  Pallas kernels  77 us (98%)
    pallas_call x1, Pallas kernels, on_device(): pl.pallas_call(kernel, out_shape=pltpu.VMEM((6, 2048), BF), in_specs=[hbm...  77 us

profile of v2, /device:TPU:6, one launch (start us, length us, event | category | flops | bytes accessed | tf_op | source)
XLA Modules:
  0.0 77.7 jit_solution(8249090718167426475)
XLA Ops:
  0.0 77.0 %layer.1 = bf16[6,2048]{1,0:T(8,128)(2,1)S(1)} custom-call(bf16[24,2048]{1,0:T(8,128)(2,1)} %res_hbm.1, bf16[24,256]{1,0:T(8,128)(2,1)} %q_hbm.1, bf16[24,256]{1,0:T(8,128)(2,1)} %k_hbm.1, bf16[24,512]{1,0:T(8,128)(2,1)} %v_hbm.1, bf16[24,512]{1,0:T(8,128)(2,1)} %og_hbm.1, f32[4,24]{1,0:T(4,128)} %bitcast.11, f32[4,24]{1,0:T(4,128)} %bitcast.12, ...), custom_call_target="tpu_custom_call" | custom-call | tf_op jit(solution)/shard_map/layer/pallas_call | solution.py:482
  77.0 0.6 copy.21

commit v3 on v2

--- a/solution.py
+++ b/solution.py
@@ -22,8 +22,9 @@
 DIRECT = (-6, 5, -3, 3, -1, 1)
 RELAY = {-2: -1, 2: 1, -4: -3, -5: -3, 4: 3, 6: 5, 7: 5, -7: -6, -8: -6}
 REACH = (-6, -5, -3, -2, -1, 1, 2, 3, 5, 6)
-LEAVES = ((-4, -2, 2), (-8, -7, 7, 6, -5, 4))
-N_SEM = 128
+BLOCKS = 4
+LEAVES = ((-2,), (-4, 2), (-5, 4), (-8, -7, 7, 6))
+N_SEM = 192
 GATE_AT, DECAY_AT, BETA_AT = 16, 32, 40
 
 
@@ -116,7 +117,8 @@
     NT[GATE_AT : GATE_AT + TOPK, 0:ROWS] = eg_ref[...]
     NT[DECAY_AT : DECAY_AT + HEADS, 0:ROWS] = di_ref[...]
     NT[BETA_AT : BETA_AT + HEADS, 0:ROWS] = bi_ref[...]
-    MG[0] = jnp.transpose(NT[...])[0:ROWS]
+    narrow = jnp.transpose(NT[...])[0:ROWS]
+    MG[0] = jnp.concatenate([narrow[8 * g : 8 * g + 8, 0:32] for g in range(3)] + [jnp.zeros((8, 32), F32)], axis=1)
     pl.semaphore_wait(barrier, len(peers))
 
     def direct(buf):
@@ -134,7 +136,6 @@
 
     for copy in heads:
         copy.wait()
-    narrow = MG[0]
     q_unit, k_unit, cross = [], [], []
     for g in range(2):
         for ref, scale, units, base in ((q_ref, 128 ** (-0.5), q_unit, 0), (k_ref, 1.0, k_unit, 2)):
@@ -185,7 +186,7 @@
         if k:
             moved_a[k] = remote(AP.at[k], AR.at[k - 1], at_x(k))
 
-    for via in (-1, 1, -3, 3):
+    for via in (-1, 1, -3, 3, 5, -6):
         relay(MG, meta, via)
 
     for k in (1, 3, 2):
@@ -204,196 +205,207 @@
         moved_w.append(remote(up_hbm.at[0, x_cols(k), :], W.at[x, :, pl.ds(128, 128)], at_x(k)))
     moved_d = [remote(dp_hbm.at[0, :, x_cols(k)], D.at[x], at_x(k)) for k in (2, 1, 3)]
 
-    for via in (5, -6):
-        relay(MG, meta, via)
+    for via in (-1, 1):
+        relay(G, rows_z, via)
     for delta in RELAY:
         meta[delta].wait_recv()
     lane = iota((ROWS, 128), 1)
-    lane_expert = jnp.where(lane < 32, 16 * z + lane // 2, -1).astype(F32)
+    lane_expert = jnp.where(lane < 32, 16 * z + (lane >> 1), -1).astype(F32)[0:8]
 
     def name_slots(i):
         for u in range(4):
             j = 4 * i + u
             info = MG[j]
-            match = jnp.zeros((ROWS, 128), F32)
-            gates = jnp.zeros((ROWS, 128), F32)
-            for k in range(TOPK):
-                same = info[:, k : k + 1] == lane_expert
-                match = jnp.where(same, 1.0, match)
-                gates = jnp.where(same, info[:, GATE_AT + k : GATE_AT + k + 1], gates)
-            at = pl.ds(pl.multiple_of(j * ROWS, 8), ROWS)
-            MT[at, :] = match
-            GT[at, :] = gates
+            for g in range(3):
+                match = jnp.zeros((8, 128), F32)
+                gates = jnp.zeros((8, 128), F32)
+                for k in range(TOPK):
+                    same = info[:, 32 * g + k : 32 * g + k + 1] == lane_expert
+                    match = jnp.where(same, 1.0, match)
+                    gates = jnp.where(same, info[:, 32 * g + GATE_AT + k : 32 * g + GATE_AT + k + 1], gates)
+                at = pl.ds(pl.multiple_of(j * ROWS + 8 * g, 8), 8)
+                MT[at, :] = match
+                GT[at, :] = gates
 
     pl.loop(0, 4)(name_slots)
-    half = 8 * ROWS
-    row_a, row_b = iota((half, half), 0), iota((half, half), 1)
-    lower = ((row_a > row_b) & (row_a // ROWS == row_b // ROWS)).astype(F32).astype(BF)
-    spread = (
-        (iota((128, 256), 0) // 2 == iota((128, 256), 1) // 16)
-        & (iota((128, 256), 0) % 2 == (iota((128, 256), 1) // 8) % 2)
-    )
+    later_row = (iota((ROWS, ROWS), 0) > iota((ROWS, ROWS), 1)).astype(F32).astype(BF)
+    lane_c, lane_w = iota((128, 128), 0), iota((128, 128), 1)
+    spread = ((lane_c >> 1) == (lane_w >> 3)) & ((lane_c & 1) == ((lane_w >> 2) & 1))
     spread = spread.astype(F32).astype(BF)
-    lane_slot = (iota((half, 128), 1) % 2).astype(F32)
-    lane_place = iota((half, 256), 1) % 8
-    def place_slots(h):
-        match = MT[half * h : half * h + half, :]
-        earlier = dot(lower, match.astype(BF))
-        here = jnp.where(earlier == lane_slot, match, 0.0)
-        gates = here * GT[half * h : half * h + half, :]
-        GM[8 * h : 8 * h + 8, :] = jnp.concatenate(
-            [jnp.sum(gates[ROWS * j : ROWS * j + ROWS], axis=0, keepdims=True) for j in range(8)], axis=0
-        )
-        placed = jnp.where(lane_place == iota((half, 256), 0) // ROWS, dot(here.astype(BF), spread), 0.0)
-        none = jnp.zeros((ROWS, 256), F32)
-        for j in range(8):
-            one = placed[ROWS * j : ROWS * j + ROWS]
-            PTL[h, j] = jnp.concatenate([one, none], axis=0).astype(BF)
-            PTR[h, j] = jnp.concatenate([none, one], axis=0).astype(BF)
-        PL[h] = jnp.transpose(PTL[h].reshape(8 * CH, 256).astype(F32)).astype(BF)
-        PR[h] = jnp.transpose(PTR[h].reshape(8 * CH, 256).astype(F32)).astype(BF)
-
-    moved_y = []
-
-    def select(h):
-        for delta in ORDER[8 * h : 8 * h + 8]:
-            if delta and delta not in RELAY.values():
-                rows_z[delta].wait_recv()
-        chunks = G[8 * h : 8 * h + 8].reshape(8 * CH, CW)
-        S[h, :, :, :, 0:CW] = dot(PL[h], chunks).astype(BF).reshape(8, 2, 16, CW)
-        S[h, :, :, :, CW:DX] = dot(PR[h], chunks).astype(BF).reshape(8, 2, 16, CW)
-        moved_y.append([remote(S.at[h, ds[k]], R.at[h, :, me], at_y(k)) for k in range(1, 8)])
-        for p in range(2):
-            R[h, p, me] = S[h, me, p]
-
-    moved_m = []
-
-    def products(h):
-        for copy in moved_y[h]:
-            copy.wait_recv()
-        for p in range(2):
-            block = R[h, p].reshape(128, DX)
-            for t in range(2):
-                MS[h, 2 * p + t] = dot(block, W[2 * p + t]).astype(BF)
-            plain = block.astype(F32) * inverse
-            squares = jnp.sum(plain * plain, axis=1, keepdims=True)
-            SSB[h, p] = jnp.transpose(jnp.broadcast_to(squares, (128, 128)))[0:8]
-        moved = []
-        for k in (2, 1, 3):
-            moved.append(remote(MS.at[h, xs[k]], MR.at[h, k - 1], at_x(k)))
-            moved.append(remote(SSB.at[h, xs[k] // 2], SSR.at[h, k - 1], at_x(k)))
-        moved_m.append(moved)
-
-    moved_i = []
-
-    def activate(h):
-        for copy in moved_m[h]:
-            copy.wait_recv()
-        both = (MS[h, x].astype(F32) + MR[h, 0].astype(F32)) + (MR[h, 1].astype(F32) + MR[h, 2].astype(F32))
-        squares = (SSB[h, x // 2] + SSR[h, 0]) + (SSR[h, 1] + SSR[h, 2])
-        squares = jnp.transpose(jnp.concatenate([squares] * 16, axis=0))[:, 0:1]
-        scale = lax.rsqrt(squares * (1.0 / 2048.0) + 1e-06)
-        gate = both[:, 0:128] * scale
-        up = both[:, 128:256] * scale
-        IN[h, x] = (gate * sigmoid(gate) * up).astype(BF)
-        moved_i.append([remote(IN.at[h, x], IN.at[h, x], at_x(k)) for k in (2, 1, 3)])
-
-    moved_r = []
-
-    def down(h):
-        if h == 0:
-            for copy in moved_d:
-                copy.wait_recv()
-        for copy in moved_i[h]:
-            copy.wait_recv()
-        for p in range(2):
-            inner = jnp.concatenate([IN[h, 2 * p], IN[h, 2 * p + 1]], axis=1)
-            part = dot(inner, D[2 * p : 2 * p + 2].reshape(256, DX))
-            weight = KW[h, p]
-            part = part * jnp.concatenate([weight] * 4, axis=1)
-            Y[h, :, p] = part.astype(BF).reshape(8, 16, DX)
-        moved_r.append([remote(Y.at[h, ds[k]], R2.at[h, me], at_y(k)) for k in range(1, 8)])
-        R2[h, me] = Y[h, me]
-
-    def combine(h):
-        for copy in moved_r[h]:
-            copy.wait_recv()
-        back = R2[h].reshape(256, DX)
-        left = dot(PTL[h].reshape(8 * CH, 256), back[:, 0:CW])
-        right = dot(PTR[h].reshape(8 * CH, 256), back[:, CW:DX])
-        C[8 * h : 8 * h + 8] = (left + right).reshape(8, CH, CW)
-
-    back_z = {}
-
-    def give(delta, via):
-        place = PLACE[delta]
-        back_z[delta] = remote(CB.at[place], T.at[place], at_z(delta - via))
-
-    def leaves(h):
-        for delta in LEAVES[h]:
-            CB[PLACE[delta]] = C[PLACE[delta]].astype(BF)
-            give(delta, RELAY[delta])
-
-    def weigh():
-        for copy in moved_g:
-            copy.wait_recv()
-        slot_gate = GS[...].reshape(128, 128)
-        taken = (slot_gate > 0.0).astype(F32).astype(BF)
-
-        def order(dim):
-            at = iota((128, 128), dim)
-            nth = at % 16
-            far = (nth + 1) // 2
-            place = (z + jnp.where(nth % 2 == 1, -far, far) + 16) % 16
-            return place * 8 + at // 16
-
-        before = (order(1) < order(0)).astype(F32).astype(BF)
-        lane_a, lane_b = iota((128, 128), 0), iota((128, 128), 1)
-        pair = (lane_a // 2 == lane_b // 2).astype(F32).astype(BF)
-        first = ((lane_a // 2 == lane_b // 2) & (lane_a < lane_b)).astype(F32).astype(BF)
-        rank = dot(before, dot(taken, pair).astype(BF)) + dot(taken, first)
-        limit_0 = cap_ref[2 * row].astype(F32)
-        limit_1 = cap_ref[2 * row + 1].astype(F32)
-        limit = jnp.where((lane_b // 2) % 2 == 0, limit_0, limit_1)
-        kept = jnp.where(rank < limit, slot_gate, 0.0)
-        for p in range(2):
-            columns = [
-                jnp.sum(jnp.where(lane_b == 4 * me + 2 * p + t, kept, 0.0), axis=1, keepdims=True) for t in range(2)
-            ]
-            for h in range(2):
-                column = jnp.concatenate(
-                    [c[16 * d + 8 * h : 16 * d + 8 * h + 8] for d in range(8) for c in columns], axis=0
-                )
-                KW[h, p] = jnp.broadcast_to(column, (128, 128))
-
-    for via in (-1, 1, -3, 3):
+    lane_slot = (lane & 1).astype(F32)
+    lane_place = lane & 3
+
+    def place_slots(b):
+        totals = []
+        for u in range(4):
+            at = slice(ROWS * (4 * b + u), ROWS * (4 * b + u) + ROWS)
+            match = MT[at, :]
+            here = jnp.where(dot(later_row, match.astype(BF)) == lane_slot, match, 0.0)
+            totals.append(jnp.sum(here * GT[at, :], axis=0, keepdims=True))
+            placed = jnp.where(lane_place == u, dot(here.astype(BF), spread), 0.0)
+            none = jnp.zeros((ROWS, 128), F32)
+            PTL[b, u] = jnp.concatenate([placed, none], axis=0).astype(BF)
+            PTR[b, u] = jnp.concatenate([none, placed], axis=0).astype(BF)
+        GM[8 * b : 8 * b + 8, :] = jnp.concatenate(totals * 2, axis=0)
+        PL[b] = jnp.transpose(PTL[b].reshape(4 * CH, 128).astype(F32)).astype(BF)
+        PR[b] = jnp.transpose(PTR[b].reshape(4 * CH, 128).astype(F32)).astype(BF)
+
+    for via in (-3, 3):
         relay(G, rows_z, via)
     place_slots(0)
     for via in (5, -6):
         relay(G, rows_z, via)
+    moved_y = []
+
+    def select(b):
+        for delta in ORDER[4 * b : 4 * b + 4]:
+            if delta and delta not in RELAY.values():
+                rows_z[delta].wait_recv()
+        chunks = G[4 * b : 4 * b + 4].reshape(4 * CH, CW)
+        S[b, :, :, 0:CW] = dot(PL[b], chunks).astype(BF).reshape(8, 16, CW)
+        S[b, :, :, CW:DX] = dot(PR[b], chunks).astype(BF).reshape(8, 16, CW)
+        moved_y.append([remote(S.at[b, ds[k]], R.at[b, me], at_y(k)) for k in (4, 5, 3, 2, 6, 7, 1)])
+        R[b, me] = S[b, me]
+
+    moved_m = []
+
+    def products(b):
+        for copy in moved_y[b]:
+            copy.wait_recv()
+        block = R[b].reshape(128, DX)
+        for t in range(4):
+            both = dot(block, W[t]).reshape(8, 2, 8, 256)[:, t // 2]
+            MS[b, t] = both.reshape(64, 256).astype(BF)
+        plain = block.astype(F32) * inverse
+        squares = jnp.sum(plain * plain, axis=1, keepdims=True)
+        SSB[b] = jnp.transpose(jnp.broadcast_to(squares, (128, 128)))[0:8]
+        moved = []
+        for k in (2, 1, 3):
+            moved.append(remote(MS.at[b, xs[k]], MR.at[b, k - 1], at_x(k)))
+            moved.append(remote(SSB.at[b], SSR.at[b, k - 1], at_x(k)))
+        moved_m.append(moved)
+
+    moved_i = []
+
+    def activate(b):
+        for copy in moved_m[b]:
+            copy.wait_recv()
+        both = (MS[b, x].astype(F32) + MR[b, 0].astype(F32)) + (MR[b, 1].astype(F32) + MR[b, 2].astype(F32))
+        squares = (SSB[b] + SSR[b, 0]) + (SSR[b, 1] + SSR[b, 2])
+        squares = jnp.transpose(jnp.concatenate([squares] * 16, axis=0))[:, 0:1].reshape(8, 2, 8, 1)
+        squares = jnp.where(x // 2 == 0, squares[:, 0], squares[:, 1]).reshape(64, 1)
+        scale = lax.rsqrt(squares * (1.0 / 2048.0) + 1e-06)
+        gate = both[:, 0:128] * scale
+        up = both[:, 128:256] * scale
+        IN[b, x] = (gate * sigmoid(gate) * up).astype(BF)
+        moved_i.append([remote(IN.at[b, x], IN.at[b, x], at_x(k)) for k in (2, 1, 3)])
+
+    moved_r = []
+
+    def down(b):
+        if b == 0:
+            for copy in moved_d:
+                copy.wait_recv()
+        for copy in moved_i[b]:
+            copy.wait_recv()
+        parts = []
+        for p in range(2):
+            inner = jnp.concatenate([IN[b, 2 * p], IN[b, 2 * p + 1]], axis=1)
+            part = dot(inner, D[2 * p : 2 * p + 2].reshape(256, DX))
+            part = part * jnp.concatenate([KW[b, p]] * 4, axis=1)
+            parts.append(part.reshape(8, 8, DX))
+        Y[b] = jnp.concatenate(parts, axis=1).astype(BF)
+        moved_r.append([remote(Y.at[b, ds[k]], R2.at[b, me], at_y(k)) for k in (4, 5, 3, 2, 6, 7, 1)])
+        R2[b, me] = Y[b, me]
+
+    def combine(b):
+        for copy in moved_r[b]:
+            copy.wait_recv()
+        back = R2[b].reshape(128, DX)
+        left = dot(PTL[b].reshape(4 * CH, 128), back[:, 0:CW])
+        right = dot(PTR[b].reshape(4 * CH, 128), back[:, CW:DX])
+        C[4 * b : 4 * b + 4] = (left + right).reshape(4, CH, CW)
+
+    back_z = {}
+
+    def give(delta, via):
+        place = PLACE[delta]
+        back_z[delta] = remote(CB.at[place], T.at[place], at_z(delta - via))
+
+    def leaves(b):
+        for delta in LEAVES[b]:
+            CB[PLACE[delta]] = C[PLACE[delta]].astype(BF)
+            give(delta, RELAY[delta])
+
+    def weigh():
+        for copy in moved_g:
+            copy.wait_recv()
+        slot_gate = GS[...].reshape(256, 128)
+        taken = (slot_gate > 0.0).astype(F32).astype(BF)
+
+        def order(at):
+            nth = ((at >> 3) & 3) * 4 + (at & 3)
+            far = (nth + 1) >> 1
+            place = (z + jnp.where((nth & 1) == 1, -far, far) + 16) & 15
+            return place * 8 + (at >> 5)
+
+        to, source = iota((256, 256), 0), iota((256, 256), 1)
+        before = ((order(source) < order(to)) & ((source & 4) == 0)).astype(F32).astype(BF)
+        pair = (lane_c >> 1) == (lane_w >> 1)
+        first = (pair & (lane_c < lane_w)).astype(F32).astype(BF)
+        pair = pair.astype(F32).astype(BF)
+        rank = dot(before, dot(taken, pair).astype(BF)) + dot(taken, first)
+        limit_0 = cap_ref[2 * row].astype(F32)
+        limit_1 = cap_ref[2 * row + 1].astype(F32)
+        lanes = iota((256, 128), 1)
+        limit = jnp.where(((lanes >> 1) & 1) == 0, limit_0, limit_1)
+        kept = jnp.where(rank < limit, slot_gate, 0.0)
+        second = (iota((256, 1), 0) & 4) != 0
+        for p in range(2):
+            slots = [
+                jnp.sum(jnp.where(lanes == 4 * me + 2 * p + t, kept, 0.0), axis=1, keepdims=True) for t in range(2)
+            ]
+            column = jnp.where(second, slots[1], slots[0])
+            for b in range(BLOCKS):
+                piece = jnp.concatenate([column[32 * d + 8 * b : 32 * d + 8 * b + 8] for d in range(8)], axis=0)
+                KW[b, p] = jnp.broadcast_to(piece, (64, 128))
+
     select(0)
     place_slots(1)
     select(1)
+    place_slots(2)
+    select(2)
+    place_slots(3)
     GS[me] = GM[...]
     moved_g = [remote(GM, GS.at[me], at_y(k)) for k in range(1, 8)]
-
+    select(3)
     for copy in own_w:
         copy.wait()
     for copy in moved_w:
         copy.wait_recv()
     products(0)
     products(1)
+    products(2)
+    weigh()
     activate(0)
-    weigh()
+    products(3)
     activate(1)
     down(0)
+    activate(2)
     down(1)
+    activate(3)
+    down(2)
     combine(0)
     leaves(0)
+    down(3)
     combine(1)
     leaves(1)
-
-    for via in (-6, 5, -3, 3, -1, 1):
+    combine(2)
+    leaves(2)
+    combine(3)
+    leaves(3)
+
+    for via in (-1, 1, 3, -3, 5, -6):
         total = C[PLACE[via]]
         for delta, v in RELAY.items():
             if v == via:
@@ -445,31 +457,31 @@
         pltpu.VMEM((4, DX, DX), BF),
         pltpu.VMEM((4, DX, 256), BF),
         pltpu.VMEM((4, 128, DX), BF),
-        pltpu.VMEM((16, ROWS, 128), F32),
+        pltpu.VMEM((16, 8, 128), F32),
         pltpu.VMEM((2, 8 * ROWS, 128), F32),
         pltpu.VMEM((HEADS, 8 * ROWS, 128), F32),
         pltpu.VMEM((4, ROWS, DX), F32),
         pltpu.VMEM((3, ROWS, DX), F32),
         pltpu.VMEM((CH, CW), F32),
         pltpu.VMEM((16, CH, CW), BF),
-        pltpu.VMEM((2, 8, CH, 256), BF),
-        pltpu.VMEM((2, 8, CH, 256), BF),
-        pltpu.VMEM((2, 256, 8 * CH), BF),
-        pltpu.VMEM((2, 256, 8 * CH), BF),
-        pltpu.VMEM((2, 8, 2, 16, DX), BF),
-        pltpu.VMEM((2, 2, 8, 16, DX), BF),
+        pltpu.VMEM((BLOCKS, 4, CH, 128), BF),
+        pltpu.VMEM((BLOCKS, 4, CH, 128), BF),
+        pltpu.VMEM((BLOCKS, 128, 4 * CH), BF),
+        pltpu.VMEM((BLOCKS, 128, 4 * CH), BF),
+        pltpu.VMEM((BLOCKS, 8, 16, DX), BF),
+        pltpu.VMEM((BLOCKS, 8, 16, DX), BF),
         pltpu.VMEM((16 * ROWS, 128), F32),
         pltpu.VMEM((16 * ROWS, 128), F32),
-        pltpu.VMEM((16, 128), F32),
-        pltpu.VMEM((8, 16, 128), F32),
-        pltpu.VMEM((2, 2, 128, 128), F32),
-        pltpu.VMEM((2, 4, 128, 256), BF),
-        pltpu.VMEM((2, 3, 128, 256), BF),
-        pltpu.VMEM((2, 2, 8, 128), F32),
-        pltpu.VMEM((2, 3, 8, 128), F32),
-        pltpu.VMEM((2, 4, 128, 128), BF),
-        pltpu.VMEM((2, 8, 2, 16, DX), BF),
-        pltpu.VMEM((2, 8, 2, 16, DX), BF),
+        pltpu.VMEM((32, 128), F32),
+        pltpu.VMEM((8, 32, 128), F32),
+        pltpu.VMEM((BLOCKS, 2, 64, 128), F32),
+        pltpu.VMEM((BLOCKS, 4, 64, 256), BF),
+        pltpu.VMEM((BLOCKS, 3, 64, 256), BF),
+        pltpu.VMEM((BLOCKS, 8, 128), F32),
+        pltpu.VMEM((BLOCKS, 3, 8, 128), F32),
+        pltpu.VMEM((BLOCKS, 4, 64, 128), BF),
+        pltpu.VMEM((BLOCKS, 8, 16, DX), BF),
+        pltpu.VMEM((BLOCKS, 8, 16, DX), BF),
         pltpu.VMEM((16, CH, CW), F32),
         pltpu.VMEM((16, CH, CW), BF),
         pltpu.VMEM((16, CH, CW), BF),

time: 78.3 us -> 75 us (0.958)
  the two profiles are of different devices: /device:TPU:6 before, /device:TPU:8 now
where the time goes in v3:
time: 75 us; the launch traced here: 74.9 us
  Pallas kernels  74.3 us (99%)
    pallas_call x1, Pallas kernels, on_device(): pl.pallas_call(kernel, out_shape=pltpu.VMEM((6, 2048), BF), in_specs=[hbm...  74.3 us

profile of v3, /device:TPU:8, one launch (start us, length us, event | category | flops | bytes accessed | tf_op | source)
XLA Modules:
  0.0 74.9 jit_solution(15622350568813398806)
XLA Ops:
  0.0 74.3 %layer.1 = bf16[6,2048]{1,0:T(8,128)(2,1)S(1)} custom-call(bf16[24,2048]{1,0:T(8,128)(2,1)} %res_hbm.1, bf16[24,256]{1,0:T(8,128)(2,1)} %q_hbm.1, bf16[24,256]{1,0:T(8,128)(2,1)} %k_hbm.1, bf16[24,512]{1,0:T(8,128)(2,1)} %v_hbm.1, bf16[24,512]{1,0:T(8,128)(2,1)} %og_hbm.1, f32[4,24]{1,0:T(4,128)} %bitcast.11, f32[4,24]{1,0:T(4,128)} %bitcast.12, ...), custom_call_target="tpu_custom_call" | custom-call | tf_op jit(solution)/shard_map/layer/pallas_call | solution.py:494
  74.3 0.6 copy.21

commit v4 on v3

--- a/solution.py
+++ b/solution.py
@@ -119,7 +119,6 @@
     NT[BETA_AT : BETA_AT + HEADS, 0:ROWS] = bi_ref[...]
     narrow = jnp.transpose(NT[...])[0:ROWS]
     MG[0] = jnp.concatenate([narrow[8 * g : 8 * g + 8, 0:32] for g in range(3)] + [jnp.zeros((8, 32), F32)], axis=1)
-    pl.semaphore_wait(barrier, len(peers))
 
     def direct(buf):
         return {a: remote(buf.at[0], buf.at[PLACE[a]], at_z(-a)) for a in DIRECT}
@@ -130,9 +129,6 @@
             if v == via:
                 copies[delta] = remote(buf.at[PLACE[v]], buf.at[PLACE[delta]], at_z(v - delta))
 
-    meta = direct(MG)
-
-    moved_w = [remote(gp_hbm.at[0, x_cols(k), :], W.at[x, :, pl.ds(0, 128)], at_x(k)) for k in (1, 3)]
 
     for copy in heads:
         copy.wait()
@@ -161,6 +157,9 @@
     for copy in states:
         copy.wait()
     pl.loop(0, ROWS // STEP)(read_rows)
+    pl.semaphore_wait(barrier, len(peers))
+    meta = direct(MG)
+    moved_w = [remote(gp_hbm.at[0, x_cols(k), :], W.at[x, :, pl.ds(0, 128)], at_x(k)) for k in (1, 3)]
 
     gated = []
     for h in range(HEADS):
@@ -186,7 +185,7 @@
         if k:
             moved_a[k] = remote(AP.at[k], AR.at[k - 1], at_x(k))
 
-    for via in (-1, 1, -3, 3, 5, -6):
+    for via in (-1, 1, -3, 3):
         relay(MG, meta, via)
 
     for k in (1, 3, 2):
@@ -205,7 +204,9 @@
         moved_w.append(remote(up_hbm.at[0, x_cols(k), :], W.at[x, :, pl.ds(128, 128)], at_x(k)))
     moved_d = [remote(dp_hbm.at[0, :, x_cols(k)], D.at[x], at_x(k)) for k in (2, 1, 3)]
 
-    for via in (-1, 1):
+    for via in (5, -6):
+        relay(MG, meta, via)
+    for via in (-1, 1, -3, 3):
         relay(G, rows_z, via)
     for delta in RELAY:
         meta[delta].wait_recv()
@@ -250,8 +251,6 @@
         PL[b] = jnp.transpose(PTL[b].reshape(4 * CH, 128).astype(F32)).astype(BF)
         PR[b] = jnp.transpose(PTR[b].reshape(4 * CH, 128).astype(F32)).astype(BF)
 
-    for via in (-3, 3):
-        relay(G, rows_z, via)
     place_slots(0)
     for via in (5, -6):
         relay(G, rows_z, via)
@@ -386,18 +385,18 @@
     products(0)
     products(1)
     products(2)
+    products(3)
     weigh()
     activate(0)
-    products(3)
     activate(1)
+    activate(2)
+    activate(3)
     down(0)
-    activate(2)
     down(1)
-    activate(3)
     down(2)
+    down(3)
     combine(0)
     leaves(0)
-    down(3)
     combine(1)
     leaves(1)
     combine(2)

time: 75 us -> 74 us (0.987)
  the two profiles are of different devices: /device:TPU:8 before, /device:TPU:6 now
where the time goes in v4:
time: 74 us; the launch traced here: 73.9 us
  Pallas kernels  73.3 us (99%)
    pallas_call x1, Pallas kernels, on_device(): pl.pallas_call(kernel, out_shape=pltpu.VMEM((6, 2048), BF), in_specs=[hbm...  73.3 us

profile of v4, /device:TPU:6, one launch (start us, length us, event | category | flops | bytes accessed | tf_op | source)
XLA Modules:
  0.0 73.9 jit_solution(9304141545242473567)
XLA Ops:
  0.0 73.3 %layer.1 = bf16[6,2048]{1,0:T(8,128)(2,1)S(1)} custom-call(bf16[24,2048]{1,0:T(8,128)(2,1)} %res_hbm.1, bf16[24,256]{1,0:T(8,128)(2,1)} %q_hbm.1, bf16[24,256]{1,0:T(8,128)(2,1)} %k_hbm.1, bf16[24,512]{1,0:T(8,128)(2,1)} %v_hbm.1, bf16[24,512]{1,0:T(8,128)(2,1)} %og_hbm.1, f32[4,24]{1,0:T(4,128)} %bitcast.11, f32[4,24]{1,0:T(4,128)} %bitcast.12, ...), custom_call_target="tpu_custom_call" | custom-call | tf_op jit(solution)/shard_map/layer/pallas_call | solution.py:493
  73.3 0.6 copy.21
